TPU v7x, 512 devices: a whole 4x8x8 slice. The times are simulated.
512 devices in a mesh: prow: 32 (over x, z), pcol: 16 (over y, core).
Axes of the slice: x: 4, y: 8, z: 8, core: 2. Of those that a mesh axis runs over, the one named last changes fastest.
Arguments:
- sym_matrix: float32 [14336, 14336], P('prow', 'pcol'), may hold values from -4 to 4, as said below
- panel: float32 [14336, 128], P('prow', 'pcol'), may hold values from -0.06681531 to 0.06681531, as said below
Outputs:
- trailing: float32 [14336, 14336], P('prow', 'pcol')
- band_block: float32 [128, 128], replicated
Inputs may be any that keep to these rules, and one draw needn't show every extreme that they name: `sym_matrix`: exactly symmetric. `panel`: of full column rank.
All inputs are finite; a program needn't handle non-finite values.
Results may differ from a plain program's by a relative error of at most 0.0001.
Values sent between devices are 32-bit elements; how exact they have to be, the bound alone decides.
No kernel may reach another device: no remote copies, remote signals or barrier semaphores. Data moves between devices by JAX's collectives and lax.ppermute only.
A program may use at most 64 MiB of HBM per device.

v0:
```python
import jax
import jax.numpy as jnp
from jax import lax
from jax.sharding import PartitionSpec as P

PRECISE = lax.Precision.HIGHEST
LU_STEP = 16


def spread(block, axis, owner):
    block = jnp.where(lax.axis_index(axis) == owner, block, jnp.zeros_like(block))
    return lax.psum(block, axis)


def matmul(left_operand, right_operand):
    return jnp.dot(
        left_operand, right_operand, precision=PRECISE, preferred_element_type=jnp.float32
    )


def contract_first(left_operand, right_operand):
    return lax.dot_general(
        left_operand,
        right_operand,
        (((0,), (0,)), ((), ())),
        precision=PRECISE,
        preferred_element_type=jnp.float32,
    )


def cholesky_lower(gram_matrix):
    size_small = gram_matrix.shape[0]
    positions = jnp.arange(size_small, dtype=jnp.int32)

    def step(column_at, state):
        work, lower = state
        pivot = jnp.sqrt(work[column_at, column_at])
        column = jnp.where(positions >= column_at, work[:, column_at] / pivot, 0.0)
        trail = jnp.where(positions > column_at, column, 0.0)
        work = work - trail[:, None] * trail[None, :]
        lower = jnp.where((positions == column_at)[None, :], column[:, None], lower)
        return (work, lower)

    return lax.fori_loop(0, size_small, step, (gram_matrix, jnp.zeros_like(gram_matrix)))[1]


def solve_upper(upper, right_hand):
    size_small = upper.shape[0]
    positions = jnp.arange(size_small, dtype=jnp.int32)

    def step(count, solved):
        row_at = size_small - 1 - count
        row = jnp.where(positions > row_at, upper[row_at], 0.0)
        value = (right_hand[row_at] - matmul(row, solved)) / upper[row_at, row_at]
        return solved.at[row_at].set(value)

    return lax.fori_loop(0, size_small, step, jnp.zeros_like(right_hand))


def solve_unit_lower(lower, right_hand):
    size_small = lower.shape[0]
    positions = jnp.arange(size_small, dtype=jnp.int32)

    def step(row_at, solved):
        row = jnp.where(positions < row_at, lower[row_at], 0.0)
        value = right_hand[row_at] - matmul(row, solved)
        return solved.at[row_at].set(value)

    return lax.fori_loop(0, size_small, step, jnp.zeros_like(right_hand))


def eliminate_tall(tall):
    row_pos = jnp.arange(tall.shape[0], dtype=jnp.int32)
    col_pos = jnp.arange(tall.shape[1], dtype=jnp.int32)

    def eliminate(column_at, packed):
        pivot_value = packed[column_at, column_at]
        column = jnp.where(row_pos > column_at, packed[:, column_at] / pivot_value, 0.0)
        pivot_row = jnp.where(col_pos > column_at, packed[column_at, :], 0.0)
        packed = packed - column[:, None] * pivot_row[None, :]
        below = (col_pos[None, :] == column_at) & (row_pos[:, None] > column_at)
        return jnp.where(below, column[:, None], packed)

    return lax.fori_loop(0, tall.shape[1], eliminate, tall)


def factor_lower_upper(square):
    order_small = square.shape[0]
    width = min(LU_STEP, order_small)
    packed = square
    for start in range(0, order_small, width):
        finish = start + width
        tall = eliminate_tall(packed[start:, start:finish])
        packed = packed.at[start:, start:finish].set(tall)
        if finish < order_small:
            diag_part = tall[:width]
            small_pos = jnp.arange(width, dtype=jnp.int32)
            unit_lower = jnp.where(
                small_pos[:, None] > small_pos[None, :], diag_part, 0.0
            ) + jnp.eye(width, dtype=square.dtype)
            right_rows = solve_unit_lower(unit_lower, packed[start:finish, finish:])
            packed = packed.at[start:finish, finish:].set(right_rows)
            packed = packed.at[finish:, finish:].add(-matmul(tall[width:], right_rows))
    positions = jnp.arange(order_small, dtype=jnp.int32)
    identity = jnp.eye(order_small, dtype=square.dtype)
    lower_l = jnp.where(positions[:, None] > positions[None, :], packed, 0.0) + identity
    upper_u = jnp.where(positions[:, None] <= positions[None, :], packed, 0.0)
    return (lower_l, upper_u)


def factor_panel(gram_matrix, top_rows):
    order_small = gram_matrix.shape[0]
    identity = jnp.eye(order_small, dtype=gram_matrix.dtype)
    upper_r = -cholesky_lower(gram_matrix).T
    inverse_r = solve_upper(upper_r, identity)
    lower_l, upper_u = factor_lower_upper(identity - matmul(top_rows, inverse_r))
    inverse_u = solve_upper(upper_u, identity)
    combine = matmul(inverse_r, inverse_u)
    tfactor = solve_unit_lower(lower_l, upper_u.T).T
    return (upper_r, lower_l, combine, tfactor)


def local(sym_matrix, panel):
    row_count = sym_matrix.shape[0]
    col_count = sym_matrix.shape[1]
    block_ratio = lax.axis_size("prow") // lax.axis_size("pcol")
    prow_index = lax.axis_index("prow")
    pcol_index = lax.axis_index("pcol")
    panel_rows = lax.all_gather(panel, "pcol", axis=1, tiled=True)
    panel_width = panel_rows.shape[1]
    gram_part = contract_first(panel_rows, panel_rows)
    top_part = jnp.where(prow_index == 0, panel_rows[:panel_width], 0.0)
    gram_matrix, top_rows = lax.psum((gram_part, top_part), "prow")
    upper_r, lower_l, combine, tfactor = factor_panel(gram_matrix, top_rows)
    row_ids = prow_index * row_count + jnp.arange(row_count, dtype=jnp.int32)
    lower_rows = jnp.concatenate(
        [lower_l, jnp.zeros((row_count - panel_width, panel_width), jnp.float32)], 0
    )
    vec_rows = jnp.where((row_ids < panel_width)[:, None], lower_rows, -matmul(panel_rows, combine))
    gathered = lax.all_gather(vec_rows, "prow", axis=0, tiled=True)
    vec_cols = lax.dynamic_slice_in_dim(gathered, pcol_index * col_count, col_count, 0)
    product_part = contract_first(sym_matrix, vec_rows)
    product_cols = lax.psum(product_part, "prow")
    curvature = lax.psum(contract_first(vec_cols, product_cols), "pcol")
    middle = matmul(tfactor.T, matmul(curvature, tfactor))
    update_cols = matmul(product_cols, tfactor) - 0.5 * matmul(vec_cols, middle)
    row_share = lax.dynamic_slice_in_dim(
        update_cols, prow_index % block_ratio * row_count, row_count, 0
    )
    update_rows = spread(row_share, "pcol", prow_index // block_ratio)
    left_factor = jnp.concatenate([vec_rows, update_rows], 1)
    right_factor = jnp.concatenate([update_cols, vec_cols], 1)
    correction = lax.dot_general(
        left_factor,
        right_factor,
        (((1,), (1,)), ((), ())),
        precision=PRECISE,
        preferred_element_type=jnp.float32,
    )
    trailing = sym_matrix - correction
    return (trailing, upper_r)


def solution(mesh):
    in_specs = (P("prow", "pcol"), P("prow", "pcol"))
    out_specs = (P("prow", "pcol"), P())
    return jax.shard_map(local, mesh=mesh, in_specs=in_specs, out_specs=out_specs, check_vma=False)
```

profile of v0, /device:TPU:1, one launch (start us, length us, event | category | flops | bytes accessed | tf_op | source)
XLA Modules:
  0.0 1985.2 jit_solution(6389143411159502851)
XLA Ops:
  7.2 21.9 %all_gather.6 = f32[448,128]{0,1:T(8,128)S(1)} all-gather(f32[448,8]{0,1:T(8,128)} %param.105), channel_id=1, replica_groups=mesh['prow'=32,'pcol'=16] {'pcol'}, dimensions={1}, use_global_device_ids=true | all-gather | bytes 243712 | tf_op jit(solution)/shard_map/all_gather | solution.py:129
  32.9 145.3 %all-reduce.13.cloned.1.call-done = (f32[128,128]{1,0:T(8,128)}, f32[128,128]{1,0:T(8,128)}) async-done(((f32[128,128]{1,0:T(8,128)}, f32[128,128]{1,0:T(8,128)}), (f32[128,128]{1,0:T(8,128)}, f32[128,128]{1,0:T(8,128)})) %all-reduce.13.cloned.1.call-update) | async-done | bytes 131088 | tf_op jit(solution)/shard_map/psum | solution.py:133
  179.2 197.6 %while.332 = (s32[]{:T(128)}, f32[128,128]{0,1:T(8,128)S(1)}, f32[128,128]{1,0:T(8,128)S(1)}, s32[]{:T(128)}, s32[]{:T(128)}) while((s32[]{:T(128)}, f32[128,128]{0,1:T(8,128)S(1)}, f32[128,128]{1,0:T(8,128)S(1)}, s32[]{:T(128)}, s32[]{:T(128)}) %tuple.762), condition=%wide.region_3.4_spmd.clone.clone, body=%wide.region_2.3_spmd.clone.clone.sunk | while | flops 67075 | bytes 268659 | solution.py:44
  376.9 356.8 %while.314 = (s32[]{:T(128)}, f32[128,128]{1,0:T(8,128)S(1)}, f32[128,128]{1,0:T(8,128)S(1)}, f32[128,128]{1,0:T(8,128)S(1)}, s32[]{:T(128)}, /*index=5*/s32[2]{...) while((s32[]{:T(128)}, f32[128,128]{1,0:T(8,128)S(1)}, f32[128,128]{1,0:T(8,128)S(1)}, ...), condition=%wide.region_6.7_spmd.clone, body=%wide.region_4.6_spmd.clone.sunk | while | flops 197263 | bytes 70848 | solution.py:57
  378.3 1.4 fusion.285
  381.1 1.4 fusion.285
  383.8 1.4 fusion.285
  386.6 1.4 fusion.285
  389.4 1.4 fusion.285
  392.2 1.4 fusion.285
  395.0 1.4 fusion.285
  397.8 1.4 fusion.285
  400.6 1.4 fusion.285
  408.9 1.4 fusion.285
  420.1 1.4 fusion.285
  439.6 1.4 fusion.285
  450.7 1.4 fusion.285
  461.9 1.4 fusion.285
  473.1 1.4 fusion.285
  492.6 1.4 fusion.285
  503.7 1.4 fusion.285
  514.9 1.4 fusion.285
  526.0 1.4 fusion.285
  545.5 1.4 fusion.285
  556.7 1.4 fusion.285
  567.8 1.4 fusion.285
  579.0 1.4 fusion.285
  598.5 1.4 fusion.285
  609.7 1.4 fusion.285
  620.8 1.4 fusion.285
  632.0 1.4 fusion.285
  651.5 1.4 fusion.285
  662.6 1.4 fusion.285
  673.8 1.4 fusion.285
  684.9 1.4 fusion.285
  704.4 1.4 fusion.285
  715.6 1.4 fusion.285
  726.8 1.4 fusion.285
  734.1 23.4 %while.324 = (s32[]{:T(128)}, f32[128,16]{0,1:T(8,128)S(1)}, s32[]{:T(128)}) while((s32[]{:T(128)}, f32[128,16]{0,1:T(8,128)S(1)}, s32[]{:T(128)}) %tuple.768), condition=%wide.region_9.10_spmd.clone.clone, body=%wide.region_8.9_spmd.clone.clone.sunk | while | flops 8754 | bytes 36909 | solution.py:84
  758.8 25.1 %while.315 = (s32[]{:T(128)}, f32[16,112]{1,0:T(8,128)S(1)}, f32[16,112]{1,0:T(8,128)S(1)}, f32[16,16]{1,0:T(8,128)S(1)}, s32[]{:T(128)}, /*index=5*/s32[2]{0:T(128)S(1)}, s32[1]{0:T(128)}, s32[]{:T(128)}) while((s32[]{:T(128)}, f32[16,112]{1,0:T(8,128)S(1)}, f32[16,112]{1,0:T(8,128)S(1)}, f32[16,16]{1,0:T(8,128)S(1)}, ...), condition=%wide.region_13.14_spmd.clone, body=%wide.region_11.13_spmd.clone.sunk | while | flops 21771 | bytes 13234 | solution.py:69
  783.9 1.9 dynamic-slice_select_fusion.1
  785.8 2.0 scatter.91
  788.2 23.4 %while.325 = (s32[]{:T(128)}, f32[112,16]{0,1:T(8,128)S(1)}, s32[]{:T(128)}) while((s32[]{:T(128)}, f32[112,16]{0,1:T(8,128)S(1)}, s32[]{:T(128)}) %tuple.774), condition=%wide.region_15.16_spmd.clone.clone, body=%wide.region_14.15_spmd.clone.clone.sunk | while | flops 7666 | bytes 32589 | solution.py:84
  814.3 26.4 %while.316 = (s32[]{:T(128)}, f32[16,96]{1,0:T(8,128)S(1)}, f32[16,96]{1,0:T(8,128)S(1)}, f32[16,16]{1,0:T(8,128)S(1)}, s32[]{:T(128)}, /*index=5*/s32[2]{0:T(128)S(1)}, s32[1]{0:T(128)}, s32[]{:T(128)}) while((s32[]{:T(128)}, f32[16,96]{1,0:T(8,128)S(1)}, f32[16,96]{1,0:T(8,128)S(1)}, f32[16,16]{1,0:T(8,128)S(1)}, s32[]{:T(128)}, ...), condition=%wide.region_18.19_spmd.clone, body=%wide.region_16.18_spmd.clone.sunk | while | flops 18667 | bytes 13042 | solution.py:69
  843.1 23.3 %while.326 = (s32[]{:T(128)}, f32[96,16]{0,1:T(8,128)S(1)}, s32[]{:T(128)}) while((s32[]{:T(128)}, f32[96,16]{0,1:T(8,128)S(1)}, s32[]{:T(128)}) %tuple.780), condition=%wide.region_20.21_spmd.clone.clone, body=%wide.region_19.20_spmd.clone.clone.sunk | while | flops 6578 | bytes 28269 | solution.py:84
  867.7 26.4 %while.317 = (s32[]{:T(128)}, f32[16,80]{1,0:T(8,128)S(1)}, f32[16,80]{1,0:T(8,128)S(1)}, f32[16,16]{1,0:T(8,128)S(1)}, s32[]{:T(128)}, /*index=5*/s32[2]{0:T(128)S(1)}, s32[1]{0:T(128)}, s32[]{:T(128)}) while((s32[]{:T(128)}, f32[16,80]{1,0:T(8,128)S(1)}, f32[16,80]{1,0:T(8,128)S(1)}, f32[16,16]{1,0:T(8,128)S(1)}, s32[]{:T(128)}, ...), condition=%wide.region_23.24_spmd.clone, body=%wide.region_21.23_spmd.clone.sunk | while | flops 15563 | bytes 12850 | solution.py:69
  896.4 23.2 %while.327 = (s32[]{:T(128)}, f32[80,16]{0,1:T(8,128)S(1)}, s32[]{:T(128)}) while((s32[]{:T(128)}, f32[80,16]{0,1:T(8,128)S(1)}, s32[]{:T(128)}) %tuple.786), condition=%wide.region_25.26_spmd.clone.clone, body=%wide.region_24.25_spmd.clone.clone.sunk | while | flops 5490 | bytes 23949 | solution.py:84
  920.9 26.4 %while.318 = (s32[]{:T(128)}, f32[16,64]{1,0:T(8,128)S(1)}, f32[16,64]{1,0:T(8,128)S(1)}, f32[16,16]{1,0:T(8,128)S(1)}, s32[]{:T(128)}, /*index=5*/s32[2]{0:T(128)S(1)}, s32[1]{0:T(128)}, s32[]{:T(128)}) while((s32[]{:T(128)}, f32[16,64]{1,0:T(8,128)S(1)}, f32[16,64]{1,0:T(8,128)S(1)}, f32[16,16]{1,0:T(8,128)S(1)}, s32[]{:T(128)}, ...), condition=%wide.region_28.29_spmd.clone, body=%wide.region_26.28_spmd.clone.sunk | while | flops 12459 | bytes 12658 | solution.py:69
  949.5 23.1 %while.328 = (s32[]{:T(128)}, f32[64,16]{0,1:T(8,128)S(1)}, s32[]{:T(128)}) while((s32[]{:T(128)}, f32[64,16]{0,1:T(8,128)S(1)}, s32[]{:T(128)}) %tuple.792), condition=%wide.region_30.31_spmd.clone.clone, body=%wide.region_29.30_spmd.clone.clone.sunk | while | flops 4402 | bytes 19629 | solution.py:84
  973.8 26.4 %while.319 = (s32[]{:T(128)}, f32[16,48]{1,0:T(8,128)S(1)}, f32[16,48]{1,0:T(8,128)S(1)}, f32[16,16]{1,0:T(8,128)S(1)}, s32[]{:T(128)}, /*index=5*/s32[2]{0:T(128)S(1)}, s32[1]{0:T(128)}, s32[]{:T(128)}) while((s32[]{:T(128)}, f32[16,48]{1,0:T(8,128)S(1)}, f32[16,48]{1,0:T(8,128)S(1)}, f32[16,16]{1,0:T(8,128)S(1)}, s32[]{:T(128)}, ...), condition=%wide.region_33.34_spmd.clone, body=%wide.region_31.33_spmd.clone.sunk | while | flops 9355 | bytes 12466 | solution.py:69
  1002.3 23.0 %while.329 = (s32[]{:T(128)}, f32[48,16]{0,1:T(8,128)S(1)}, s32[]{:T(128)}) while((s32[]{:T(128)}, f32[48,16]{0,1:T(8,128)S(1)}, s32[]{:T(128)}) %tuple.798), condition=%wide.region_35.36_spmd.clone.clone, body=%wide.region_34.35_spmd.clone.clone.sunk | while | flops 3314 | bytes 15309 | solution.py:84
  1026.5 26.4 %while.320 = (s32[]{:T(128)}, f32[16,32]{1,0:T(8,128)S(1)}, f32[16,32]{1,0:T(8,128)S(1)}, f32[16,16]{1,0:T(8,128)S(1)}, s32[]{:T(128)}, /*index=5*/s32[2]{0:T(128)S(1)}, s32[1]{0:T(128)}, s32[]{:T(128)}) while((s32[]{:T(128)}, f32[16,32]{1,0:T(8,128)S(1)}, f32[16,32]{1,0:T(8,128)S(1)}, f32[16,16]{1,0:T(8,128)S(1)}, s32[]{:T(128)}, ...), condition=%wide.region_38.39_spmd.clone, body=%wide.region_36.38_spmd.clone.sunk | while | flops 6251 | bytes 12274 | solution.py:69
  1054.9 22.9 %while.330 = (s32[]{:T(128)}, f32[32,16]{0,1:T(8,128)S(1)}, s32[]{:T(128)}) while((s32[]{:T(128)}, f32[32,16]{0,1:T(8,128)S(1)}, s32[]{:T(128)}) %tuple.804), condition=%wide.region_40.41_spmd.clone.clone, body=%wide.region_39.40_spmd.clone.clone.sunk | while | flops 2226 | bytes 10989 | solution.py:84
  1078.8 26.4 %while.321 = (s32[]{:T(128)}, f32[16,16]{1,0:T(8,128)S(1)}, f32[16,16]{1,0:T(8,128)S(1)}, f32[16,16]{1,0:T(8,128)S(1)}, s32[]{:T(128)}, /*index=5*/s32[2]{0:T(128)S(1)}, s32[1]{0:T(128)}, s32[]{:T(128)}) while((s32[]{:T(128)}, f32[16,16]{1,0:T(8,128)S(1)}, f32[16,16]{1,0:T(8,128)S(1)}, f32[16,16]{1,0:T(8,128)S(1)}, s32[]{:T(128)}, ...), condition=%wide.region_43.44_spmd.clone, body=%wide.region_41.43_spmd.clone.sunk | while | flops 3147 | bytes 12082 | solution.py:69
  1107.1 22.7 %while.331 = (s32[]{:T(128)}, f32[16,16]{0,1:T(8,128)S(1)}, s32[]{:T(128)}) while((s32[]{:T(128)}, f32[16,16]{0,1:T(8,128)S(1)}, s32[]{:T(128)}) %tuple.810), condition=%wide.region_45.46_spmd.clone.clone, body=%wide.region_44.45_spmd.clone.clone.sunk | while | flops 1138 | bytes 6665 | solution.py:84
  1130.8 361.7 %while.322 = (s32[]{:T(128)}, f32[128,128]{1,0:T(8,128)S(1)}, f32[128,128]{1,0:T(8,128)S(1)}, f32[128,128]{1,0:T(8,128)S(1)}, s32[]{:T(128)}, /*index=5*/s32[2]{...) while((s32[]{:T(128)}, f32[128,128]{1,0:T(8,128)S(1)}, f32[128,128]{1,0:T(8,128)S(1)}, ...), condition=%wide.region_48.49_spmd.clone, body=%wide.region_46.48_spmd.clone.sunk | while | flops 197263 | bytes 70848 | solution.py:57
  1494.2 2.8 convolution_bitcast_fusion.10
  1497.1 210.2 %while.323 = (s32[]{:T(128)}, f32[128,128]{1,0:T(8,128)S(1)}, f32[128,128]{1,0:T(8,128)S(1)}, f32[128,128]{1,0:T(8,128)S(1)}, s32[]{:T(128)}, /*index=5*/s32[2]{0:T(128)S(1)}, s32[1]{0:T(128)}, s32[]{:T(128)}) while((s32[]{:T(128)}, f32[128,128]{1,0:T(8,128)S(1)}, f32[128,128]{1,0:T(8,128)S(1)}, f32[128,128]{1,0:T(8,128)S(1)}, ...), condition=%wide.region_52.53_spmd.clone, body=%wide.region_50.52_spmd.clone.sunk | while | flops 197131 | bytes 70770 | solution.py:69
  1708.4 44.1 %all-reduce.7.cloned.1.call-done = f32[896,128]{0,1:T(8,128)} async-done(((f32[896,128]{0,1:T(8,128)}), f32[896,128]{0,1:T(8,128)}) %all-reduce.7.cloned.1.call-update) | async-done | bytes 458768 | tf_op jit(solution)/shard_map/psum | solution.py:143
  1752.5 2.6 fusion.194
  1755.2 1.9 fusion.193
  1757.1 104.1 %all-reduce.9.cloned.1.call-done = f32[128,128]{1,0:T(8,128)} async-done(((f32[128,128]{1,0:T(8,128)}), f32[128,128]{1,0:T(8,128)}) %all-reduce.9.cloned.1.call-update) | async-done | bytes 65552 | tf_op jit(solution)/shard_map/psum | solution.py:144
  1863.8 111.0 %all-reduce.11.cloned.1.call-done = f32[448,128]{1,0:T(8,128)} async-done(((f32[448,128]{1,0:T(8,128)}), f32[448,128]{1,0:T(8,128)}) %all-reduce.11.cloned.1.call-update) | async-done | bytes 229392 | tf_op jit(solution)/shard_map/psum | solution.py:12
  1974.8 3.8 convolution_subtract_fusion
  (3608 shorter events, 1370.4 us)
Async XLA Ops:
  7.2 171.0 %all-reduce.13.cloned.1.call-start = ((), (), s32[]{:S(2)}) async-start(), calls=%async_computation.4 | async-start | bytes 262144 | tf_op jit(solution)/shard_map/psum | solution.py:133
  29.1 347.8 %copy-start.3 = (s32[2]{0:T(128)S(1)}, s32[2]{0:T(128)}, u32[]{:S(2)}) copy-start(s32[2]{0:T(128)} %constant.1551.clone.2) | copy-start | bytes 28
  30.9 1676.5 %all-gather.2.cloned.1.call-start = ((), (), s32[]{:S(2)}) async-start(), calls=%async_computation.1 | async-start | bytes 7569408 | tf_op jit(solution)/shard_map/all_gather | solution.py:140
  178.2 555.6 %copy-start.5 = (f32[128,128]{1,0:T(8,128)S(1)}, f32[128,128]{1,0:T(8,128)}, u32[]{:S(2)}) copy-start(f32[128,128]{1,0:T(8,128)} %get-tuple-element.2758) | copy-start | bytes 196612
  179.2 579.6 %copy-start.2 = (s32[2]{0:T(128)S(1)}, s32[2]{0:T(128)}, u32[]{:S(2)}) copy-start(s32[2]{0:T(128)} %constant.1562.clone.2) | copy-start | bytes 28
  733.8 109.2 %copy-start.4 = (f32[128,128]{1,0:T(8,128)}, f32[128,128]{1,0:T(8,128)S(1)}, u32[]{:S(2)}) copy-start(f32[128,128]{1,0:T(8,128)S(1)} %get-tuple-element.3520) | copy-start | bytes 196612
  1077.9 416.3 %copy-start = (f32[448,896]{1,0:T(8,128)S(1)}, f32[448,896]{1,0:T(8,128)}, u32[]{:S(2)}) copy-start(f32[448,896]{1,0:T(8,128)} %param.104) | copy-start | bytes 4816900
  1494.0 258.5 %all-reduce.7.cloned.1.call-start = ((), (), s32[]{:S(2)}) async-start(), calls=%async_computation | async-start | bytes 917504 | tf_op jit(solution)/shard_map/psum | solution.py:143
  1497.1 364.2 %all-reduce.9.cloned.1.call-start = ((), (), s32[]{:S(2)}) async-start(), calls=%async_computation.2 | async-start | bytes 131072 | tf_op jit(solution)/shard_map/psum | solution.py:144
  1755.1 219.7 %all-reduce.11.cloned.1.call-start = ((), (), s32[]{:S(2)}) async-start(), calls=%async_computation.3 | async-start | bytes 458752 | tf_op jit(solution)/shard_map/psum | solution.py:12
  1755.2 219.7 %copy-start.1 = (f32[448,128]{1,0:T(8,128)S(1)}, f32[448,128]{1,0:T(8,128)}, u32[]{:S(2)}) copy-start(f32[448,128]{1,0:T(8,128)} %fusion.165) | copy-start | bytes 688132
Sparse Core Ops, SparseCore 0:
  31.0 147.1 all-reduce.12
  1494.1 101.8 all-gather.1
  1600.4 152.1 all-reduce.6
  1755.3 105.9 all-reduce.8
  1864.1 110.6 all-reduce.10
where the time goes:
time: 1990 us
  matrix products  573 us (29%)
  other arithmetic  504 us (25%)
  waiting for transfers between devices  405 us (20%)
  local copies, waits for them, and re-layouts  356 us (18%)
  loops' own time  111 us (6%)
  blocking collectives  21.9 us (1%)
    dot_general x510, matrix products, matmul(): jnp.dot(left_operand, right_operand, precision=PRECISE, preferred_element...  562 us
    another operation x500, other arithmetic  382 us
    dynamic_slice x256, local copies, waits for them, and re-layouts, step(): value = (right_hand[row_at] - matmul(row, solved)) / upper[row_at, row_at]  154 us
    psum x1, waiting for transfers between devices, local(): gram_matrix, top_rows = lax.psum((gram_part, top_part), 'prow')  145 us
    psum x1, waiting for transfers between devices, spread(): return lax.psum(block, axis)  111 us
    psum x1, waiting for transfers between devices, local(): curvature = lax.psum(contract_first(vec_cols, product_cols), 'pcol')  104 us
    another operation x1, loops' own time, cholesky_lower(): lax.fori_loop(0, size_small, step, (gram_matrix, jnp.zeros_like(gram_matr...  96.7 us
    broadcast_in_dim x128, other arithmetic, eliminate(): return jnp.where(below, column[:, None], packed)  83.7 us
  transfers between devices with their start and end apart: 5, of which 4 were waited for; matrix products, arithmetic and copies ran while one was open for 11% of the time, Pallas kernels for 0%

commit v1 on v0

v1 whole, which is shorter than its diff:
```python
import jax
import jax.numpy as jnp
from jax import lax
from jax.experimental import pallas as pl
from jax.experimental.pallas import tpu as pltpu
from jax.sharding import PartitionSpec as P

PRECISE = lax.Precision.HIGHEST
VMEM_BYTES = 48 * 2**20
NB = 128
SUB = 8


def mm(left, right, contract=((1,), (0,))):
    return lax.dot_general(
        left, right, (contract, ((), ())), precision=PRECISE, preferred_element_type=jnp.float32
    )


def lane_ceil(count):
    return -(-count // NB) * NB


NT = ((1,), (1,))
TN = ((0,), (0,))


def first_rows_zeroed(block, is_first):
    lanes = lax.broadcasted_iota(jnp.int32, block.shape, 1)
    return jnp.where(is_first & (lanes < NB), 0.0, block)


def product_kernel(panels, matrix, sent):
    cols = matrix.shape[1]
    is_first = lax.axis_index("prow") == 0
    keep = jnp.where(is_first, 1.0, 0.0)
    own = pl.ds(pl.multiple_of(lax.axis_index("pcol") * SUB, SUB), SUB)
    rows_t = panels[:, cols:]
    part = mm(first_rows_zeroed(rows_t, is_first), matrix[...])
    gram = mm(panels[own, cols:], rows_t, NT)
    top = panels[own, cols : cols + NB] * keep
    half = NB // SUB
    for dest in range(half):
        sent[dest, :, :cols] = part[dest * SUB : (dest + 1) * SUB]
        sent[dest + half, :, :cols] = matrix[dest * SUB : (dest + 1) * SUB, :] * keep
    for dest in range(2 * half):
        sent[dest, :, cols : cols + NB] = gram
        sent[dest, :, cols + NB :] = top


def reduce_kernel(got, panels, sent):
    cols = panels.shape[1] - panels.shape[1] // 3
    is_first = lax.axis_index("pcol") == 0
    total = jnp.sum(got[...], axis=0)
    small = mm(total[:, :cols], first_rows_zeroed(panels[:, :cols], is_first), NT)
    corner = total[:, :NB] * jnp.where(is_first, 1.0, 0.0)
    for dest in range(sent.shape[0]):
        sent[dest, :, : cols + 2 * NB] = total
        sent[dest, :, cols + 2 * NB : cols + 3 * NB] = small
        sent[dest, :, cols + 3 * NB :] = corner


def spread_kernel(got, sent, gram, top_t):
    parts = got.shape[0]
    cols = got.shape[2] - 4 * NB
    rows = cols // 2
    at = lane_ceil(cols + rows)
    own = got[lax.axis_index("pcol"), :, :cols]
    corner = jnp.sum(got[:, :, cols + 2 * NB :], axis=0)
    for part in range(parts):
        gram[part * SUB : (part + 1) * SUB, :] = got[part, :, cols : cols + NB]
        top_t[part * SUB : (part + 1) * SUB, :] = got[part, :, cols + NB : cols + 2 * NB]
        whole = got[part, :, :cols]
        for half in range(2):
            dest = 2 * part + half
            sent[dest, :, :cols] = own
            sent[dest, :, cols : cols + rows] = whole[:, half * rows : (half + 1) * rows]
            sent[dest, :, cols + rows : at] = jnp.zeros((SUB, at - cols - rows), jnp.float32)
            sent[dest, :, at:] = corner


def factor_kernel(gram, top_t, band, inv_s, lower, tfac, work, inv_c, rest, inv_l, upper):
    rows = lax.broadcasted_iota(jnp.int32, (NB, NB), 0)
    lanes = lax.broadcasted_iota(jnp.int32, (NB, NB), 1)
    lane = lax.broadcasted_iota(jnp.int32, (1, NB), 1)
    eye = jnp.where(rows == lanes, 1.0, 0.0)
    work[...] = gram[...]
    rest[...] = -top_t[...].T
    inv_c[...] = eye
    inv_l[...] = eye
    inv_s[...] = eye
    scales = jnp.zeros((1, NB), jnp.float32)
    for k in range(NB):
        lo = (k // SUB) * SUB
        hi = lo + SUB
        below = rows[lo:, :1] > k
        inv = lax.rsqrt(work[k : k + 1, k : k + 1])
        c_row = jnp.where(lane >= k, work[k : k + 1, :] * inv, 0.0)
        band[k : k + 1, :] = -c_row
        c_col = jnp.where(below, work[lo:, k : k + 1] * inv, 0.0)
        x_row = inv_c[k : k + 1, :] * inv
        s_row = jnp.where(lane >= k, rest[k : k + 1, :] - c_row, 0.0)
        scale = 1.0 / (rest[k : k + 1, k : k + 1] - c_row[:, k : k + 1])
        l_col = jnp.where(below, rest[lo:, k : k + 1] * scale, 0.0)
        l_row = inv_l[k : k + 1, :]
        right = jnp.where(lane > k, s_row, 0.0)
        upper[k : k + 1, :] = s_row
        scales = jnp.where(lane == k, scale, scales)
        work[lo:, :] = work[lo:, :] - c_col * c_row
        inv_c[lo:, :] = jnp.where(rows[lo:] == k, x_row, inv_c[lo:, :] - c_col * x_row)
        rest[lo:, :] = rest[lo:, :] - l_col * right
        inv_l[lo:, :] = inv_l[lo:, :] - l_col * l_row
        s_col = inv_s[:hi, k : k + 1] * scale
        inv_s[:hi, :] = jnp.where(lanes[:hi] == k, s_col, inv_s[:hi, :] - s_col * right)
    lower[...] = jnp.where(rows > lanes, rest[...] * scales, eye)
    tfac[...] = -mm(upper[...], mm(inv_l[...], inv_c[...]), NT)


def update_kernel(panels, got, matrix, inv_s, lower, tfac, out):
    rows, cols = matrix.shape
    combine = -inv_s[...]
    low = lower[...]
    t = tfac[...]
    mix = jnp.concatenate([combine, low], 0)
    moved = got[:, : cols + rows]
    corner = got[:, lane_ceil(cols + rows) :]
    prod_t = mm(mix, moved, TN)
    curv = mm(mm(mix, corner, TN), mix)
    mid = mm(t, mm(curv, t), TN)
    is_row, is_col = lax.axis_index("prow") == 0, lax.axis_index("pcol") == 0
    vec_cols = mm(combine, first_rows_zeroed(panels[:, :cols], is_col), TN)
    vec_rows = mm(combine, first_rows_zeroed(panels[:, cols:], is_row), TN)
    low_t = low.T
    vec_cols = jnp.concatenate(
        [vec_cols[:, :NB] + low_t * jnp.where(is_col, 1.0, 0.0), vec_cols[:, NB:]], 1
    )
    vec_rows = jnp.concatenate(
        [vec_rows[:, :NB] + low_t * jnp.where(is_row, 1.0, 0.0), vec_rows[:, NB:]], 1
    )
    upd_t = mm(t, prod_t, TN)
    upd_cols = upd_t[:, :cols] - 0.5 * mm(mid, vec_cols, TN)
    upd_rows = upd_t[:, cols:] - 0.5 * mm(mid, vec_rows, TN)
    left = jnp.concatenate([vec_rows, upd_rows], 0)
    right = jnp.concatenate([upd_cols, vec_cols], 0)
    out[...] = matrix[...] - mm(left, right, TN)


def call(kernel, shapes, *args, scratch=(), cost=None):
    outs = [jax.ShapeDtypeStruct(s, jnp.float32) for s in shapes]
    return pl.pallas_call(
        kernel,
        out_shape=outs,
        scratch_shapes=[pltpu.VMEM(s, jnp.float32) for s in scratch],
        compiler_params=pltpu.CompilerParams(vmem_limit_bytes=VMEM_BYTES),
        cost_estimate=cost,
    )(*args)


def exchange(blocks, axis):
    return lax.all_to_all(blocks, axis, 0, 0)


def local(matrix, panel):
    rows, cols = matrix.shape
    n_row, n_col = lax.axis_size("prow"), lax.axis_size("pcol")
    block_t = panel.T
    column = exchange(jnp.broadcast_to(block_t[None], (n_row, SUB, rows)), "prow")
    column = column.reshape(n_col, 2, SUB, rows).transpose(0, 2, 1, 3).reshape(n_col, SUB, cols)
    own = jnp.broadcast_to(block_t[None], (n_col, SUB, rows))
    panels = exchange(jnp.concatenate([column, own], 2), "pcol").reshape(NB, cols + rows)
    (sent,) = call(product_kernel, [(n_row, SUB, cols + 2 * NB)], panels, matrix)
    (sent,) = call(reduce_kernel, [(n_col, SUB, cols + 4 * NB)], exchange(sent, "prow"), panels)
    wide = lane_ceil(cols + rows) + 2 * NB
    sent, gram, top_t = call(
        spread_kernel,
        [(n_row, SUB, wide), (NB, NB), (NB, NB)],
        exchange(sent, "pcol"),
    )
    got = exchange(sent, "prow").reshape(2 * NB, wide)
    small = (NB, NB)
    band, inv_s, lower, tfac = call(
        factor_kernel,
        [small] * 4,
        gram,
        top_t,
        scratch=[small] * 5,
        cost=pl.CostEstimate(flops=2 * 10**10, bytes_accessed=2**20, transcendentals=0),
    )
    (trailing,) = call(update_kernel, [(rows, cols)], panels, got, matrix, inv_s, lower, tfac)
    return (trailing, band)


def solution(mesh):
    specs = (P("prow", "pcol"), P("prow", "pcol"))
    return jax.shard_map(
        local, mesh=mesh, in_specs=specs, out_specs=(P("prow", "pcol"), P()), check_vma=False
    )
```

time: 1990 us -> 183 us (0.09)
  matrix products: 573 us -> 0 us
  other arithmetic: 504 us -> 0.05 us
  waiting for transfers between devices: 405 us -> 29.3 us
  local copies, waits for them, and re-layouts: 356 us -> 4.34 us
  loops' own time: 111 us -> 0 us
  blocking collectives: 21.9 us -> 123 us
  Pallas kernels: 0 us -> 21 us
    dot_general x514 -> x0, matrix products: 573 us -> none  [the longest x510 562 us: matmul(): jnp.dot(left_operand, right_operand, precision=PRECISE, preferred_element...]
    psum x4 -> x0, waiting for transfers between devices: 405 us -> none  [the longest x1 145 us: local(): gram_matrix, top_rows = lax.psum((gram_part, top_part), 'prow')]
    another operation x500 -> x0, other arithmetic: 382 us -> none
    dynamic_slice x513 -> x0, local copies, waits for them, and re-layouts: 305 us -> none  [the longest x256 154 us: step(): value = (right_hand[row_at] - matmul(row, solved)) / upper[row_at, row_at]]
    all_to_all x0 -> x4, blocking collectives: none -> 123 us  [exchange(): return lax.all_to_all(blocks, axis, 0, 0)]
    another operation x19 -> x0, loops' own time: 111 us -> none  [the longest x1 96.7 us: cholesky_lower(): lax.fori_loop(0, size_small, step, (gram_matrix, jnp.zeros_like(gram_matr...]
    broadcast_in_dim x256 -> x0, other arithmetic: 85.6 us -> none  [the longest x128 83.7 us: eliminate(): return jnp.where(below, column[:, None], packed)]
    all_to_all x0 -> x1, waiting for transfers between devices: none -> 29.3 us  [exchange(): return lax.all_to_all(blocks, axis, 0, 0)]
  transfers between devices with their start and end apart: 5 -> 1, of which waited for: 4 -> 1; matrix products, arithmetic and copies ran while one was open for 11% -> 0% of each run, Pallas kernels for 0% -> 7%
where the time goes in v1:
time: 183 us; the launch traced here: 182 us
  blocking collectives  123 us (67%)
  waiting for transfers between devices  29.3 us (16%)
  Pallas kernels  21 us (11%)
  local copies, waits for them, and re-layouts  4.34 us (2%)
  starting transfers between devices  4.16 us (2%)
    all_to_all x4, blocking collectives, exchange(): return lax.all_to_all(blocks, axis, 0, 0)  123 us
    all_to_all x1, waiting for transfers between devices, exchange(): return lax.all_to_all(blocks, axis, 0, 0)  29.3 us
    pallas_call x5, Pallas kernels, call(): pl.pallas_call(kernel, out_shape=outs, scratch_shapes=[pltpu.VMEM(s, jnp....  21 us
    all_to_all x1, starting transfers between devices, exchange(): return lax.all_to_all(blocks, axis, 0, 0)  4.16 us
  transfers between devices with their start and end apart: 1, of which 1 were waited for; matrix products, arithmetic and copies ran while one was open for 0% of the time, Pallas kernels for 7%

profile of v1, /device:TPU:1, one launch (start us, length us, event | category | flops | bytes accessed | tf_op | source)
XLA Modules:
  0.0 182.4 jit_solution(482305755648923486)
XLA Ops:
  0.6 0.8 broadcast_in_dim.4
  1.4 0.0 copy-start.3
  1.4 27.8 %all_to_all.25 = f32[32,8,448]{2,1,0:T(8,128)S(1)} all-to-all(f32[32,8,448]{2,1,0:T(8,128)S(1)} %broadcast_in_dim.4), channel_id=1, replica_groups=mesh['prow'=32,'pcol'=16] {'prow'}, dimensions={0} | all-to-all | bytes 917504 | tf_op jit(solution)/shard_map/all_to_all | solution.py:160
  29.2 0.4 copy.4
  29.7 0.5 reshape.18
  30.2 0.0 copy-done.3
  30.2 0.0 copy-start
  30.3 32.1 %all_to_all.26 = f32[16,8,1344]{2,1,0:T(8,128)S(1)} all-to-all(f32[16,8,1344]{2,1,0:T(8,128)S(1)} %pad_maximum_fusion), channel_id=1, replica_groups=mesh['prow'=32,'pcol'=16] {'pcol'}, dimensions={0} | all-to-all | bytes 1376256 | tf_op jit(solution)/shard_map/all_to_all | solution.py:160
  62.4 0.0 copy-done
  62.4 1.3 shard_map.41
  63.7 37.8 %all_to_all.27.got = f32[32,8,1152]{2,1,0:T(8,128)S(1)} all-to-all(f32[32,8,1152]{2,1,0:T(8,128)S(1)} %shard_map.41), channel_id=1, replica_groups=mesh['prow'=32,'pcol'=16] {'prow'}, dimensions={0} | all-to-all | bytes 2359296 | tf_op jit(solution)/shard_map/all_to_all | solution.py:160
  101.4 0.6 shard_map.42
  102.0 25.1 %all_to_all.28.got = f32[16,8,1408]{2,1,0:T(8,128)S(1)} all-to-all(f32[16,8,1408]{2,1,0:T(8,128)S(1)} %shard_map.42), channel_id=1, replica_groups=mesh['prow'=32,'pcol'=16] {'pcol'}, dimensions={0} | all-to-all | bytes 1441792 | tf_op jit(solution)/shard_map/all_to_all | solution.py:160
  127.1 0.2 shard_map.43
  127.3 0.0 copy-start.2
  127.3 1.2 copy-done.2
  128.5 4.2 %all-to-all-start.4 = ((f32[32,8,1664]{2,1,0:T(8,128)}), f32[32,8,1664]{2,1,0:T(8,128)S(1)}, u32[]{:S(2)}, u32[]{:S(2)}) async-start(f32[32,8,1664]{2,1,0:T(8,128)} %copy-done.2), calls=%async_computation.4 | async-start | bytes 3407872 | tf_op jit(solution)/shard_map/all_to_all | solution.py:160
  132.7 12.7 %shard_map.44 = (f32[128,128]{1,0:T(8,128)}, f32[128,128]{1,0:T(8,128)S(1)}, f32[128,128]{1,0:T(8,128)S(1)}, f32[128,128]{1,0:T(8,128)S(1)}) custom-call(f32[128,128]{1,0:T(8,128)S(1)} %get-tuple-element.10.gram, f32[128,128]{1,0:T(8,128)S(1)} %get-tuple-element.11.top_t), custom_call_target="tpu_custom_call" | custom-call | flops 20000000000 | bytes 1048576 | tf_op jit(solution)/shard_map/pallas_call | solution.py:150
  145.4 29.3 %all-to-all-done.4 = f32[32,8,1664]{2,1,0:T(8,128)S(1)} async-done(((f32[32,8,1664]{2,1,0:T(8,128)}), f32[32,8,1664]{2,1,0:T(8,128)S(1)}, u32[]{:S(2)}, u32[]{:S(2)}) %all-to-all-start.4) | async-done | bytes 1703968 | tf_op jit(solution)/shard_map/all_to_all | solution.py:160
  174.6 0.0 copy-start.1
  174.6 1.4 copy-done.1
  176.1 6.3 %shard_map.45 = f32[448,896]{1,0:T(8,128)} custom-call(f32[128,1344]{1,0:T(8,128)S(1)} %bitcast.8, f32[256,1664]{1,0:T(8,128)S(1)} %bitcast.9, f32[448,896]{1,0:T(8,128)S(1)} %copy-done.1, f32[128,128]{1,0:T(8,128)S(1)} %get-tuple-element.12.inv_s, f32[128,128]{1,0:T(8,128)S(1)} %get-tuple-element.13.lower, f32[128,128]{1,0:T(8,128)S(1)} %get-tuple-element.14.tfac), custom_call_target="tpu_custom_call" | custom-call | tf_op jit(solution)/shard_map/pallas_call | solution.py:150
  (2 shorter events, 0.1 us)
Async XLA Ops:
  1.4 28.8 %copy-start.3 = (f32[448,8]{0,1:T(8,128)S(1)}, f32[448,8]{0,1:T(8,128)}, u32[]{:S(2)}) copy-start(f32[448,8]{0,1:T(8,128)} %param.3) | copy-start | bytes 43012
  30.2 32.2 %copy-start = (f32[448,896]{1,0:T(8,128)S(1)}, f32[448,896]{1,0:T(8,128)}, u32[]{:S(2)}) copy-start(f32[448,896]{1,0:T(8,128)} %matrix.3) | copy-start | bytes 4816900
  127.3 1.2 copy-start.2
  128.5 46.1 %all-to-all-start.4 = ((f32[32,8,1664]{2,1,0:T(8,128)}), f32[32,8,1664]{2,1,0:T(8,128)S(1)}, u32[]{:S(2)}, u32[]{:S(2)}) async-start(f32[32,8,1664]{2,1,0:T(8,128)} %copy-done.2), calls=%async_computation.4 | async-start | bytes 3407872 | tf_op jit(solution)/shard_map/all_to_all | solution.py:160
  174.6 1.4 copy-start.1

commit v2 on v1

v2 whole, which is shorter than its diff:
```python
import jax
import jax.numpy as jnp
from jax import lax
from jax.experimental import pallas as pl
from jax.experimental.pallas import tpu as pltpu
from jax.sharding import PartitionSpec as P

PRECISE = lax.Precision.HIGHEST
VMEM_BYTES = 48 * 2**20
NB = 128
SUB = 8
HALF = SUB // 2


def mm(left, right, contract=((1,), (0,))):
    return lax.dot_general(
        left, right, (contract, ((), ())), precision=PRECISE, preferred_element_type=jnp.float32
    )


def lane_ceil(count):
    return -(-count // NB) * NB


NT = ((1,), (1,))
TN = ((0,), (0,))


def first_rows_zeroed(block, is_first):
    lanes = lax.broadcasted_iota(jnp.int32, block.shape, 1)
    return jnp.where(is_first & (lanes < NB), 0.0, block)


def gram_kernel(rows_t, sent):
    own = pl.ds(pl.multiple_of(lax.axis_index("pcol") * SUB, SUB), SUB)
    block = rows_t[own, :]
    gram = mm(block, rows_t[...], NT)
    for dest in range(sent.shape[0]):
        sent[dest, :, :NB] = gram
        sent[dest, :, NB:] = block


def sort_kernel(got, small, blocks):
    rows = got.shape[2] - NB
    gram = jnp.sum(got[:, :, :NB], axis=0)
    for dest in range(small.shape[0]):
        small[dest, :, :NB] = gram
        small[dest, :, NB:] = got[0, :, NB : 2 * NB]
        blocks[dest, :, :rows] = got[2 * dest, :, NB:]
        blocks[dest, :, rows:] = got[2 * dest + 1, :, NB:]


def vectors(panel_t, combine, low, is_first):
    vec = mm(combine, first_rows_zeroed(panel_t, is_first), TN)
    head = vec[:, :NB] + low.T * jnp.where(is_first, 1.0, 0.0)
    return jnp.concatenate([head, vec[:, NB:]], 1)


def product_kernel(rows_t, matrix, inv_s, lower, vec_rows, sent):
    vec = vectors(rows_t[...], -inv_s[...], lower[...], lax.axis_index("prow") == 0)
    vec_rows[...] = vec
    part = mm(vec, matrix[...])
    for dest in range(sent.shape[0]):
        sent[dest] = part[dest * HALF : (dest + 1) * HALF]


def reduce_kernel(got, cols_t, inv_s, lower, vec_cols, sent):
    cols = cols_t.shape[1]
    vec = vectors(cols_t[...], -inv_s[...], lower[...], lax.axis_index("pcol") == 0)
    vec_cols[...] = vec
    total = jnp.sum(got[...], axis=0)
    small = mm(total, vec, NT)
    for dest in range(sent.shape[0]):
        sent[dest, :, :cols] = total
        sent[dest, :, cols:] = small


def spread_kernel(got, sent):
    cols = got.shape[2] - NB
    rows = cols // 2
    at = lane_ceil(cols + rows)
    own = got[lax.axis_index("pcol"), :, :cols]
    small = jnp.sum(got[:, :, cols:], axis=0)
    for part in range(got.shape[0]):
        whole = got[part, :, :cols]
        for half in range(2):
            dest = 2 * part + half
            sent[dest, :, :cols] = own
            sent[dest, :, cols : cols + rows] = whole[:, half * rows : (half + 1) * rows]
            sent[dest, :, cols + rows : at] = jnp.zeros((HALF, at - cols - rows), jnp.float32)
            sent[dest, :, at:] = small


def factor_kernel(got, band, inv_s, lower, tfac, work, inv_c, rest, inv_l, upper):
    rows = lax.broadcasted_iota(jnp.int32, (NB, NB), 0)
    lanes = lax.broadcasted_iota(jnp.int32, (NB, NB), 1)
    lane = lax.broadcasted_iota(jnp.int32, (1, NB), 1)
    eye = jnp.where(rows == lanes, 1.0, 0.0)
    for part in range(got.shape[0]):
        work[part * SUB : (part + 1) * SUB, :] = got[part, :, :NB]
        rest[part * SUB : (part + 1) * SUB, :] = -got[part, :, NB:]
    rest[...] = rest[...].T
    inv_c[...] = eye
    inv_l[...] = eye
    inv_s[...] = eye
    scales = jnp.zeros((1, NB), jnp.float32)
    for k in range(NB):
        lo = (k // SUB) * SUB
        hi = lo + SUB
        below = rows[lo:, :1] > k
        inv = lax.rsqrt(work[k : k + 1, k : k + 1])
        c_row = jnp.where(lane >= k, work[k : k + 1, :] * inv, 0.0)
        band[k : k + 1, :] = -c_row
        c_col = jnp.where(below, work[lo:, k : k + 1] * inv, 0.0)
        x_row = inv_c[k : k + 1, :] * inv
        s_row = jnp.where(lane >= k, rest[k : k + 1, :] - c_row, 0.0)
        scale = 1.0 / (rest[k : k + 1, k : k + 1] - c_row[:, k : k + 1])
        l_col = jnp.where(below, rest[lo:, k : k + 1] * scale, 0.0)
        l_row = inv_l[k : k + 1, :]
        right = jnp.where(lane > k, s_row, 0.0)
        upper[k : k + 1, :] = s_row
        scales = jnp.where(lane == k, scale, scales)
        work[lo:, :] = work[lo:, :] - c_col * c_row
        inv_c[lo:, :] = jnp.where(rows[lo:] == k, x_row, inv_c[lo:, :] - c_col * x_row)
        rest[lo:, :] = rest[lo:, :] - l_col * right
        inv_l[lo:, :] = inv_l[lo:, :] - l_col * l_row
        s_col = inv_s[:hi, k : k + 1] * scale
        inv_s[:hi, :] = jnp.where(lanes[:hi] == k, s_col, inv_s[:hi, :] - s_col * right)
    lower[...] = jnp.where(rows > lanes, rest[...] * scales, eye)
    tfac[...] = -mm(upper[...], mm(inv_l[...], inv_c[...]), NT)


def update_kernel(vec_rows, vec_cols, got, matrix, tfac, out, moved):
    rows, cols = matrix.shape
    at = lane_ceil(cols + rows)
    for part in range(got.shape[0]):
        moved[part * HALF : (part + 1) * HALF, :] = got[part]
    t = tfac[...]
    mid = mm(t, mm(moved[:, at:], t), TN)
    upd_cols = mm(t, moved[:, :cols], TN) - 0.5 * mm(mid, vec_cols[...])
    upd_rows = mm(t, moved[:, cols : cols + rows], TN) - 0.5 * mm(mid, vec_rows[...])
    left = jnp.concatenate([vec_rows[...], upd_rows], 0)
    right = jnp.concatenate([upd_cols, vec_cols[...]], 0)
    out[...] = matrix[...] - mm(left, right, TN)


def call(kernel, shapes, *args, scratch=(), cost=None):
    outs = [jax.ShapeDtypeStruct(s, jnp.float32) for s in shapes]
    return pl.pallas_call(
        kernel,
        out_shape=outs,
        scratch_shapes=[pltpu.VMEM(s, jnp.float32) for s in scratch],
        compiler_params=pltpu.CompilerParams(vmem_limit_bytes=VMEM_BYTES),
        cost_estimate=cost,
    )(*args)


def exchange(blocks, axis):
    return lax.all_to_all(blocks, axis, 0, 0)


def local(matrix, panel):
    rows, cols = matrix.shape
    n_row, n_col = lax.axis_size("prow"), lax.axis_size("pcol")
    block_t = jnp.broadcast_to(panel.T[None], (n_col, SUB, rows))
    rows_t = exchange(block_t, "pcol").reshape(NB, rows)
    (sent,) = call(gram_kernel, [(n_row, SUB, NB + rows)], rows_t)
    small, blocks = call(
        sort_kernel, [(n_col, SUB, 2 * NB), (n_col, SUB, cols)], exchange(sent, "prow")
    )
    band, inv_s, lower, tfac = call(
        factor_kernel,
        [(NB, NB)] * 4,
        exchange(small, "pcol"),
        scratch=[(NB, NB)] * 5,
        cost=pl.CostEstimate(flops=2 * 10**10, bytes_accessed=2**20, transcendentals=0),
    )
    cols_t = exchange(blocks, "pcol").reshape(NB, cols)
    vec_rows, sent = call(
        product_kernel, [(NB, rows), (n_row, HALF, cols)], rows_t, matrix, inv_s, lower
    )
    vec_cols, sent = call(
        reduce_kernel,
        [(NB, cols), (n_col, HALF, cols + NB)],
        exchange(sent, "prow"),
        cols_t,
        inv_s,
        lower,
    )
    wide = lane_ceil(cols + rows) + NB
    (sent,) = call(spread_kernel, [(n_row, HALF, wide)], exchange(sent, "pcol"))
    (trailing,) = call(
        update_kernel,
        [(rows, cols)],
        vec_rows,
        vec_cols,
        exchange(sent, "prow"),
        matrix,
        tfac,
        scratch=[(NB, wide)],
    )
    return (trailing, band)


def solution(mesh):
    specs = (P("prow", "pcol"), P("prow", "pcol"))
    return jax.shard_map(
        local, mesh=mesh, in_specs=specs, out_specs=(P("prow", "pcol"), P()), check_vma=False
    )
```

time: 183 us -> 158 us (0.86)
  waiting for transfers between devices: 29.3 us -> 1.46 us
  blocking collectives: 123 us -> 130 us
  local copies, waits for them, and re-layouts: 4.34 us -> 0.74 us
    all_to_all x1, waiting for transfers between devices: 29.3 us -> 1.46 us  [exchange(): return lax.all_to_all(blocks, axis, 0, 0)]
    all_to_all x4 -> x6, blocking collectives: 123 us -> 130 us  [exchange(): return lax.all_to_all(blocks, axis, 0, 0)]
    unnamed x8 -> x2, local copies, waits for them, and re-layouts: 2.63 us -> 0.01 us
    pallas_call x5 -> x7, Pallas kernels: 21 us -> 21.1 us  [call(): pl.pallas_call(kernel, out_shape=outs, scratch_shapes=[pltpu.VMEM(s, jnp....]
  transfers between devices with their start and end apart: 1 -> 1, of which waited for: 1 -> 1; matrix products, arithmetic and copies ran while one was open for 0% -> 0% of each run, Pallas kernels for 7% -> 9%
where the time goes in v2:
time: 158 us; the launch traced here: 157 us
  blocking collectives  130 us (82%)
  Pallas kernels  21.1 us (13%)
  starting transfers between devices  3.46 us (2%)
    all_to_all x6, blocking collectives, exchange(): return lax.all_to_all(blocks, axis, 0, 0)  130 us
    pallas_call x7, Pallas kernels, call(): pl.pallas_call(kernel, out_shape=outs, scratch_shapes=[pltpu.VMEM(s, jnp....  21.1 us
    all_to_all x1, starting transfers between devices, exchange(): return lax.all_to_all(blocks, axis, 0, 0)  3.46 us
  transfers between devices with their start and end apart: 1, of which 1 were waited for; matrix products, arithmetic and copies ran while one was open for 0% of the time, Pallas kernels for 9%

profile of v2, /device:TPU:1, one launch (start us, length us, event | category | flops | bytes accessed | tf_op | source)
XLA Modules:
  0.0 157.3 jit_solution(8740948497668257114)
XLA Ops:
  0.6 0.7 broadcast_in_dim.2
  1.4 21.2 %all_to_all.35 = f32[16,8,448]{2,1,0:T(8,128)S(1)} all-to-all(f32[16,8,448]{2,1,0:T(8,128)S(1)} %broadcast_in_dim.2), channel_id=1, replica_groups=mesh['prow'=32,'pcol'=16] {'pcol'}, dimensions={0} | all-to-all | bytes 458752 | tf_op jit(solution)/shard_map/all_to_all | solution.py:159
  22.5 0.4 shard_map.41
  22.9 30.7 %all_to_all.36.got = f32[32,8,576]{2,1,0:T(8,128)S(1)} all-to-all(f32[32,8,576]{2,1,0:T(8,128)S(1)} %shard_map.41), channel_id=1, replica_groups=mesh['prow'=32,'pcol'=16] {'prow'}, dimensions={0} | all-to-all | bytes 1179648 | tf_op jit(solution)/shard_map/all_to_all | solution.py:159
  53.6 0.9 shard_map.42
  54.5 13.4 %all_to_all.37.got = f32[16,8,256]{2,1,0:T(8,128)S(1)} all-to-all(f32[16,8,256]{2,1,0:T(8,128)S(1)} %get-tuple-element.12), channel_id=1, replica_groups=mesh['prow'=32,'pcol'=16] {'pcol'}, dimensions={0} | all-to-all | bytes 262144 | tf_op jit(solution)/shard_map/all_to_all | solution.py:159
  67.9 3.5 %all-to-all-start.4 = ((f32[16,8,896]{2,1,0:T(8,128)}), f32[16,8,896]{2,1,0:T(8,128)S(1)}, u32[]{:S(2)}, u32[]{:S(2)}) async-start(f32[16,8,896]{2,1,0:T(8,128)} %get-tuple-element.17), calls=%async_computation.4 | async-start | bytes 917504 | tf_op jit(solution)/shard_map/all_to_all | solution.py:159
  71.4 0.0 copy-start
  71.4 12.7 %shard_map.43 = (f32[128,128]{1,0:T(8,128)}, f32[128,128]{1,0:T(8,128)S(1)}, f32[128,128]{1,0:T(8,128)S(1)}, f32[128,128]{1,0:T(8,128)S(1)}) custom-call(f32[16,8,256]{2,1,0:T(8,128)S(1)} %all_to_all.37.got), custom_call_target="tpu_custom_call" | custom-call | flops 20000000000 | bytes 1048576 | tf_op jit(solution)/shard_map/pallas_call | solution.py:149
  84.0 0.0 copy-done
  84.0 1.4 shard_map.44
  85.4 1.5 all-to-all-done.4
  86.9 20.5 %all_to_all.38.got = f32[32,4,896]{2,1,0:T(4,128)S(1)} all-to-all(f32[32,4,896]{2,1,0:T(4,128)S(1)} %get-tuple-element.16), channel_id=1, replica_groups=mesh['prow'=32,'pcol'=16] {'prow'}, dimensions={0} | all-to-all | bytes 917504 | tf_op jit(solution)/shard_map/all_to_all | solution.py:159
  107.4 1.3 shard_map.45
  108.7 17.3 %all_to_all.39.got = f32[16,4,1024]{2,1,0:T(4,128)S(1)} all-to-all(f32[16,4,1024]{2,1,0:T(4,128)S(1)} %get-tuple-element.19), channel_id=1, replica_groups=mesh['prow'=32,'pcol'=16] {'pcol'}, dimensions={0} | all-to-all | bytes 524288 | tf_op jit(solution)/shard_map/all_to_all | solution.py:159
  125.9 0.1 shard_map.46
  126.1 26.9 %all_to_all.40.got = f32[32,4,1536]{2,1,0:T(4,128)S(1)} all-to-all(f32[32,4,1536]{2,1,0:T(4,128)S(1)} %shard_map.46), channel_id=1, replica_groups=mesh['prow'=32,'pcol'=16] {'prow'}, dimensions={0} | all-to-all | bytes 1572864 | tf_op jit(solution)/shard_map/all_to_all | solution.py:159
  153.0 4.3 %shard_map.47 = f32[448,896]{1,0:T(8,128)} custom-call(f32[128,448]{1,0:T(8,128)S(1)} %get-tuple-element.15.vec_rows, f32[128,896]{1,0:T(8,128)S(1)} %get-tuple-element.18.vec_cols, f32[32,4,1536]{2,1,0:T(4,128)S(1)} %all_to_all.40.got, f32[448,896]{1,0:T(8,128)S(1)} %copy-done, f32[128,128]{1,0:T(8,128)S(1)} %get-tuple-element.20.tfac), custom_call_target="tpu_custom_call" | custom-call | tf_op jit(solution)/shard_map/pallas_call | solution.py:149
Async XLA Ops:
  67.9 19.0 %all-to-all-start.4 = ((f32[16,8,896]{2,1,0:T(8,128)}), f32[16,8,896]{2,1,0:T(8,128)S(1)}, u32[]{:S(2)}, u32[]{:S(2)}) async-start(f32[16,8,896]{2,1,0:T(8,128)} %get-tuple-element.17), calls=%async_computation.4 | async-start | bytes 917504 | tf_op jit(solution)/shard_map/all_to_all | solution.py:159
  71.4 12.7 %copy-start = (f32[448,896]{1,0:T(8,128)S(1)}, f32[448,896]{1,0:T(8,128)}, u32[]{:S(2)}) copy-start(f32[448,896]{1,0:T(8,128)} %matrix.3) | copy-start | bytes 4816900

commit v3 on v2

--- a/solution.py
+++ b/solution.py
@@ -3,13 +3,18 @@
 from jax import lax
 from jax.experimental import pallas as pl
 from jax.experimental.pallas import tpu as pltpu
+from jax.sharding import Mesh
 from jax.sharding import PartitionSpec as P
 
 PRECISE = lax.Precision.HIGHEST
 VMEM_BYTES = 48 * 2**20
 NB = 128
 SUB = 8
-HALF = SUB // 2
+PCOL = ("y", "core")
+
+
+def pcol_index():
+    return lax.axis_index("y") * lax.axis_size("core") + lax.axis_index("core")
 
 
 def mm(left, right, contract=((1,), (0,))):
@@ -32,7 +37,7 @@
 
 
 def gram_kernel(rows_t, sent):
-    own = pl.ds(pl.multiple_of(lax.axis_index("pcol") * SUB, SUB), SUB)
+    own = pl.ds(pl.multiple_of(pcol_index() * SUB, SUB), SUB)
     block = rows_t[own, :]
     gram = mm(block, rows_t[...], NT)
     for dest in range(sent.shape[0]):
@@ -56,39 +61,41 @@
     return jnp.concatenate([head, vec[:, NB:]], 1)
 
 
-def product_kernel(rows_t, matrix, inv_s, lower, vec_rows, sent):
-    vec = vectors(rows_t[...], -inv_s[...], lower[...], lax.axis_index("prow") == 0)
-    vec_rows[...] = vec
-    part = mm(vec, matrix[...])
-    for dest in range(sent.shape[0]):
-        sent[dest] = part[dest * HALF : (dest + 1) * HALF]
-
-
-def reduce_kernel(got, cols_t, inv_s, lower, vec_cols, sent):
-    cols = cols_t.shape[1]
-    vec = vectors(cols_t[...], -inv_s[...], lower[...], lax.axis_index("pcol") == 0)
+def product_kernel(rows_t, cols_t, matrix, inv_s, lower, vec_rows, vec_cols, sent):
+    combine, low = -inv_s[...], lower[...]
+    vec_rows[...] = vectors(rows_t[...], combine, low, lax.axis_index("prow") == 0)
+    vec = vectors(cols_t[...], combine, low, pcol_index() == 0)
     vec_cols[...] = vec
+    part = mm(vec, matrix[...], NT)
+    for dest in range(sent.shape[0]):
+        sent[dest] = part[dest * SUB : (dest + 1) * SUB]
+
+
+def reduce_kernel(got, vec_rows, sent):
     total = jnp.sum(got[...], axis=0)
-    small = mm(total, vec, NT)
-    for dest in range(sent.shape[0]):
-        sent[dest, :, :cols] = total
-        sent[dest, :, cols:] = small
+    small = mm(total, vec_rows[...], NT)
+    for dest in range(sent.shape[0]):
+        sent[dest, :, :NB] = small
+        sent[dest, :, NB:] = total
 
 
 def spread_kernel(got, sent):
-    cols = got.shape[2] - NB
-    rows = cols // 2
+    rows = got.shape[2] - NB
+    cols = 2 * rows
     at = lane_ceil(cols + rows)
-    own = got[lax.axis_index("pcol"), :, :cols]
-    small = jnp.sum(got[:, :, cols:], axis=0)
-    for part in range(got.shape[0]):
-        whole = got[part, :, :cols]
-        for half in range(2):
-            dest = 2 * part + half
-            sent[dest, :, :cols] = own
-            sent[dest, :, cols : cols + rows] = whole[:, half * rows : (half + 1) * rows]
-            sent[dest, :, cols + rows : at] = jnp.zeros((HALF, at - cols - rows), jnp.float32)
-            sent[dest, :, at:] = small
+    core = lax.axis_index("core")
+    own = got[lax.axis_index("prow"), :, NB:]
+    small = jnp.sum(got[:, :, :NB], axis=0)
+    for dest in range(sent.shape[0]):
+        here = 4 * dest + 2 * core
+        there = 4 * dest + 2 * (1 - core)
+        sent[dest, :, :rows] = got[there, :, NB:]
+        sent[dest, :, rows:cols] = got[there + 1, :, NB:]
+        sent[dest, :, cols : cols + rows] = own
+        sent[dest, :, cols + rows : at] = jnp.zeros((SUB, at - cols - rows), jnp.float32)
+        sent[dest, :, at : at + NB] = small
+        sent[dest, :, at + NB : at + NB + rows] = got[here, :, NB:]
+        sent[dest, :, at + NB + rows :] = got[here + 1, :, NB:]
 
 
 def factor_kernel(got, band, inv_s, lower, tfac, work, inv_c, rest, inv_l, upper):
@@ -130,11 +137,16 @@
     tfac[...] = -mm(upper[...], mm(inv_l[...], inv_c[...]), NT)
 
 
-def update_kernel(vec_rows, vec_cols, got, matrix, tfac, out, moved):
+def update_kernel(vec_rows, vec_cols, got, partner, matrix, tfac, out, moved):
     rows, cols = matrix.shape
     at = lane_ceil(cols + rows)
+    core = lax.axis_index("core")
     for part in range(got.shape[0]):
-        moved[part * HALF : (part + 1) * HALF, :] = got[part]
+        here = pl.ds(pl.multiple_of((2 * part + core) * SUB, SUB), SUB)
+        there = pl.ds(pl.multiple_of((2 * part + 1 - core) * SUB, SUB), SUB)
+        moved[here, :cols] = got[part, :, at + NB :]
+        moved[here, cols:] = got[part, :, cols : at + NB]
+        moved[there, :] = partner[part]
     t = tfac[...]
     mid = mm(t, mm(moved[:, at:], t), TN)
     upd_cols = mm(t, moved[:, :cols], TN) - 0.5 * mm(mid, vec_cols[...])
@@ -161,9 +173,10 @@
 
 def local(matrix, panel):
     rows, cols = matrix.shape
-    n_row, n_col = lax.axis_size("prow"), lax.axis_size("pcol")
+    n_row, n_chip = lax.axis_size("prow"), lax.axis_size("y")
+    n_col = n_chip * lax.axis_size("core")
     block_t = jnp.broadcast_to(panel.T[None], (n_col, SUB, rows))
-    rows_t = exchange(block_t, "pcol").reshape(NB, rows)
+    rows_t = exchange(block_t, PCOL).reshape(NB, rows)
     (sent,) = call(gram_kernel, [(n_row, SUB, NB + rows)], rows_t)
     small, blocks = call(
         sort_kernel, [(n_col, SUB, 2 * NB), (n_col, SUB, cols)], exchange(sent, "prow")
@@ -171,30 +184,32 @@
     band, inv_s, lower, tfac = call(
         factor_kernel,
         [(NB, NB)] * 4,
-        exchange(small, "pcol"),
+        exchange(small, PCOL),
         scratch=[(NB, NB)] * 5,
         cost=pl.CostEstimate(flops=2 * 10**10, bytes_accessed=2**20, transcendentals=0),
     )
-    cols_t = exchange(blocks, "pcol").reshape(NB, cols)
-    vec_rows, sent = call(
-        product_kernel, [(NB, rows), (n_row, HALF, cols)], rows_t, matrix, inv_s, lower
-    )
-    vec_cols, sent = call(
-        reduce_kernel,
-        [(NB, cols), (n_col, HALF, cols + NB)],
-        exchange(sent, "prow"),
+    cols_t = exchange(blocks, PCOL).reshape(NB, cols)
+    vec_rows, vec_cols, sent = call(
+        product_kernel,
+        [(NB, rows), (NB, cols), (n_col, SUB, rows)],
+        rows_t,
         cols_t,
+        matrix,
         inv_s,
         lower,
     )
+    (sent,) = call(reduce_kernel, [(n_row, SUB, NB + rows)], exchange(sent, PCOL), vec_rows)
     wide = lane_ceil(cols + rows) + NB
-    (sent,) = call(spread_kernel, [(n_row, HALF, wide)], exchange(sent, "pcol"))
+    (sent,) = call(spread_kernel, [(n_chip, SUB, wide + cols)], exchange(sent, "prow"))
+    got = exchange(sent, "y")
+    partner = lax.ppermute(got[:, :, :wide], "core", [(0, 1), (1, 0)])
     (trailing,) = call(
         update_kernel,
         [(rows, cols)],
         vec_rows,
         vec_cols,
-        exchange(sent, "prow"),
+        got,
+        partner,
         matrix,
         tfac,
         scratch=[(NB, wide)],
@@ -203,7 +218,9 @@
 
 
 def solution(mesh):
-    specs = (P("prow", "pcol"), P("prow", "pcol"))
+    n_row, n_col = mesh.devices.shape
+    grid = Mesh(mesh.devices.reshape(n_row, n_col // 2, 2), ("prow",) + PCOL)
+    specs = (P("prow", PCOL), P("prow", PCOL))
     return jax.shard_map(
-        local, mesh=mesh, in_specs=specs, out_specs=(P("prow", "pcol"), P()), check_vma=False
-    )
+        local, mesh=grid, in_specs=specs, out_specs=(P("prow", PCOL), P()), check_vma=False
+    )

time: 158 us -> 160 us (1.013)
  blocking collectives: 130 us -> 124 us
  starting transfers between devices: 3.46 us -> 8.89 us
  waiting for transfers between devices: 1.46 us -> 4.18 us
    all_to_all x6, blocking collectives: 130 us -> 124 us  [exchange(): return lax.all_to_all(blocks, axis, 0, 0)]
    ppermute x0 -> x1, starting transfers between devices: none -> 5.43 us  [local(): partner = lax.ppermute(got[:, :, :wide], 'core', [(0, 1), (1, 0)])]
  transfers between devices with their start and end apart: 1 -> 2, of which waited for: 1 -> 2; matrix products, arithmetic and copies ran while one was open for 0% -> 0% of each run, Pallas kernels for 9% -> 8%
where the time goes in v3:
time: 160 us
  blocking collectives  124 us (78%)
  Pallas kernels  21 us (13%)
  starting transfers between devices  8.89 us (6%)
  waiting for transfers between devices  4.18 us (3%)
    all_to_all x6, blocking collectives, exchange(): return lax.all_to_all(blocks, axis, 0, 0)  124 us
    pallas_call x7, Pallas kernels, call(): pl.pallas_call(kernel, out_shape=outs, scratch_shapes=[pltpu.VMEM(s, jnp....  21 us
    ppermute x1, starting transfers between devices, local(): partner = lax.ppermute(got[:, :, :wide], 'core', [(0, 1), (1, 0)])  5.43 us
    all_to_all x1, starting transfers between devices, exchange(): return lax.all_to_all(blocks, axis, 0, 0)  3.46 us
  transfers between devices with their start and end apart: 2, of which 2 were waited for; matrix products, arithmetic and copies ran while one was open for 0% of the time, Pallas kernels for 8%

profile of v3, /device:TPU:1, one launch (start us, length us, event | category | flops | bytes accessed | tf_op | source)
XLA Modules:
  0.0 159.9 jit_solution(8565327232479145157)
XLA Ops:
  0.6 0.7 broadcast_in_dim.2
  1.4 21.2 %all_to_all.35 = f32[16,8,448]{2,1,0:T(8,128)S(1)} all-to-all(f32[16,8,448]{2,1,0:T(8,128)S(1)} %broadcast_in_dim.2), channel_id=1, replica_groups=mesh['prow'=32,'y'=8,'core'=2] {'y','core'}, dimensions={0} | all-to-all | bytes 458752 | tf_op jit(solution)/shard_map/all_to_all | solution.py:171
  22.5 0.4 shard_map.41
  22.9 30.7 %all_to_all.36.got = f32[32,8,576]{2,1,0:T(8,128)S(1)} all-to-all(f32[32,8,576]{2,1,0:T(8,128)S(1)} %shard_map.41), channel_id=1, replica_groups=mesh['prow'=32,'y'=8,'core'=2] {'prow'}, dimensions={0} | all-to-all | bytes 1179648 | tf_op jit(solution)/shard_map/all_to_all | solution.py:171
  53.6 0.9 shard_map.42
  54.5 13.4 %all_to_all.37.got = f32[16,8,256]{2,1,0:T(8,128)S(1)} all-to-all(f32[16,8,256]{2,1,0:T(8,128)S(1)} %get-tuple-element.12), channel_id=1, replica_groups=mesh['prow'=32,'y'=8,'core'=2] {'y','core'}, dimensions={0} | all-to-all | bytes 262144 | tf_op jit(solution)/shard_map/all_to_all | solution.py:171
  67.9 3.5 %all-to-all-start.2 = ((f32[16,8,896]{2,1,0:T(8,128)}), f32[16,8,896]{2,1,0:T(8,128)S(1)}, u32[]{:S(2)}, u32[]{:S(2)}) async-start(f32[16,8,896]{2,1,0:T(8,128)} %get-tuple-element.11), calls=%async_computation.2 | async-start | bytes 917504 | tf_op jit(solution)/shard_map/all_to_all | solution.py:171
  71.4 0.0 copy-start
  71.4 12.7 %shard_map.43 = (f32[128,128]{1,0:T(8,128)}, f32[128,128]{1,0:T(8,128)S(1)}, f32[128,128]{1,0:T(8,128)S(1)}, f32[128,128]{1,0:T(8,128)S(1)}) custom-call(f32[16,8,256]{2,1,0:T(8,128)S(1)} %all_to_all.37.got), custom_call_target="tpu_custom_call" | custom-call | flops 20000000000 | bytes 1048576 | tf_op jit(solution)/shard_map/pallas_call | solution.py:161
  84.0 2.9 %all-to-all-done.2 = f32[16,8,896]{2,1,0:T(8,128)S(1)} async-done(((f32[16,8,896]{2,1,0:T(8,128)}), f32[16,8,896]{2,1,0:T(8,128)S(1)}, u32[]{:S(2)}, u32[]{:S(2)}) %all-to-all-start.2) | async-done | bytes 458784 | tf_op jit(solution)/shard_map/all_to_all | solution.py:171
  86.9 0.0 copy-done
  86.9 2.2 %shard_map.44 = (f32[128,448]{1,0:T(8,128)S(1)}, f32[128,896]{1,0:T(8,128)S(1)}, f32[16,8,448]{2,1,0:T(8,128)S(1)}) custom-call(f32[128,448]{1,0:T(8,128)S(1)} %bitcast.4, f32[128,896]{1,0:T(8,128)S(1)} %bitcast.5, f32[448,896]{1,0:T(8,128)S(1)} %copy-done, f32[128,128]{1,0:T(8,128)S(1)} %get-tuple-element.13.inv_s, f32[128,128]{1,0:T(8,128)S(1)} %get-tuple-element.14.lower), custom_call_target="tpu_custom_call" | custom-call | tf_op jit(solution)/shard_map/pallas_call | solution.py:161
  89.1 15.5 %all_to_all.38.got = f32[16,8,448]{2,1,0:T(8,128)S(1)} all-to-all(f32[16,8,448]{2,1,0:T(8,128)S(1)} %get-tuple-element.17), channel_id=1, replica_groups=mesh['prow'=32,'y'=8,'core'=2] {'y','core'}, dimensions={0} | all-to-all | bytes 458752 | tf_op jit(solution)/shard_map/all_to_all | solution.py:171
  104.6 0.4 shard_map.45
  105.0 24.2 %all_to_all.39.got = f32[32,8,576]{2,1,0:T(8,128)S(1)} all-to-all(f32[32,8,576]{2,1,0:T(8,128)S(1)} %shard_map.45), channel_id=1, replica_groups=mesh['prow'=32,'y'=8,'core'=2] {'prow'}, dimensions={0} | all-to-all | bytes 1179648 | tf_op jit(solution)/shard_map/all_to_all | solution.py:171
  129.2 0.1 shard_map.46
  129.3 19.4 %all_to_all.40.got = f32[8,8,2432]{2,1,0:T(8,128)S(1)} all-to-all(f32[8,8,2432]{2,1,0:T(8,128)S(1)} %shard_map.46), channel_id=1, replica_groups=mesh['prow'=32,'y'=8,'core'=2] {'y'}, dimensions={0} | all-to-all | bytes 1245184 | tf_op jit(solution)/shard_map/all_to_all | solution.py:171
  148.8 5.4 %collective-permute-start = (f32[8,8,1536]{2,1,0:T(8,128)S(1)}, f32[8,8,1536]{2,1,0:T(8,128)S(1)}, u32[]{:S(2)}, u32[]{:S(2)}) collective-permute-start(f32[8,8,1536]{2,1,0:T(8,128)S(1)} %slice.4), channel_id=1, source_target_pairs={{0,1},{1,0},{2,3},{3,2},{4,5},{5,4},{6,7},{7,6},{8,9},{9,8},{10,11... | collective-permute-start | bytes 1179656 | tf_op jit(solution)/shard_map/ppermute | solution.py:205
  154.2 1.3 collective-permute-done.partner
  155.6 4.4 %shard_map.47 = f32[448,896]{1,0:T(8,128)} custom-call(f32[128,448]{1,0:T(8,128)S(1)} %get-tuple-element.15.vec_rows, f32[128,896]{1,0:T(8,128)S(1)} %get-tuple-element.16.vec_cols, f32[8,8,2432]{2,1,0:T(8,128)S(1)} %all_to_all.40.got, f32[8,8,1536]{2,1,0:T(8,128)S(1)} %collective-permute-done.partner, f32[448,896]{1,0:T(8,128)S(1)} %copy-done, ...), custom_call_target="tpu_custom_call" | custom-call | tf_op jit(solution)/shard_map/pallas_call | solution.py:161
  (1 shorter events, 0.0 us)
Async XLA Ops:
  67.9 19.0 %all-to-all-start.2 = ((f32[16,8,896]{2,1,0:T(8,128)}), f32[16,8,896]{2,1,0:T(8,128)S(1)}, u32[]{:S(2)}, u32[]{:S(2)}) async-start(f32[16,8,896]{2,1,0:T(8,128)} %get-tuple-element.11), calls=%async_computation.2 | async-start | bytes 917504 | tf_op jit(solution)/shard_map/all_to_all | solution.py:171
  71.4 15.6 %copy-start = (f32[448,896]{1,0:T(8,128)S(1)}, f32[448,896]{1,0:T(8,128)}, u32[]{:S(2)}) copy-start(f32[448,896]{1,0:T(8,128)} %matrix.3) | copy-start | bytes 4816900
  148.8 6.8 %collective-permute-start = (f32[8,8,1536]{2,1,0:T(8,128)S(1)}, f32[8,8,1536]{2,1,0:T(8,128)S(1)}, u32[]{:S(2)}, u32[]{:S(2)}) collective-permute-start(f32[8,8,1536]{2,1,0:T(8,128)S(1)} %slice.4), channel_id=1, source_target_pairs={{0,1},{1,0},{2,3},{3,2},{4,5},{5,4},{6,7},{7,6},{8,9},{9,8},{10,11... | collective-permute-start | bytes 1179656 | tf_op jit(solution)/shard_map/ppermute | solution.py:205

commit v4 on v2

--- a/solution.py
+++ b/solution.py
@@ -20,6 +20,21 @@
 
 def lane_ceil(count):
     return -(-count // NB) * NB
+
+
+def halves(block):
+    high = block.astype(jnp.bfloat16)
+    return high, (block - high.astype(jnp.float32)).astype(jnp.bfloat16)
+
+
+def mm3(left, right, contract=((1,), (0,))):
+    left_high, left_low = halves(left)
+    right_high, right_low = halves(right)
+
+    def dot(a, b):
+        return lax.dot_general(a, b, (contract, ((), ())), preferred_element_type=jnp.float32)
+
+    return dot(left_high, right_high) + (dot(left_high, right_low) + dot(left_low, right_high))
 
 
 NT = ((1,), (1,))
@@ -64,12 +79,16 @@
         sent[dest] = part[dest * HALF : (dest + 1) * HALF]
 
 
-def reduce_kernel(got, cols_t, inv_s, lower, vec_cols, sent):
-    cols = cols_t.shape[1]
-    vec = vectors(cols_t[...], -inv_s[...], lower[...], lax.axis_index("pcol") == 0)
-    vec_cols[...] = vec
+def column_kernel(cols_t, inv_s, lower, vec_cols):
+    vec_cols[...] = vectors(
+        cols_t[...], -inv_s[...], lower[...], lax.axis_index("pcol") == 0
+    )
+
+
+def reduce_kernel(got, vec_cols, sent):
+    cols = vec_cols.shape[1]
     total = jnp.sum(got[...], axis=0)
-    small = mm(total, vec, NT)
+    small = mm3(total, vec_cols[...], NT)
     for dest in range(sent.shape[0]):
         sent[dest, :, :cols] = total
         sent[dest, :, cols:] = small
@@ -136,12 +155,12 @@
     for part in range(got.shape[0]):
         moved[part * HALF : (part + 1) * HALF, :] = got[part]
     t = tfac[...]
-    mid = mm(t, mm(moved[:, at:], t), TN)
-    upd_cols = mm(t, moved[:, :cols], TN) - 0.5 * mm(mid, vec_cols[...])
-    upd_rows = mm(t, moved[:, cols : cols + rows], TN) - 0.5 * mm(mid, vec_rows[...])
-    left = jnp.concatenate([vec_rows[...], upd_rows], 0)
+    mid = mm3(t, mm3(moved[:, at:], t), TN)
+    prod = mm3(t, moved[:, : cols + rows], TN)
+    upd_cols = prod[:, :cols] - mm3(0.5 * (mid + mid.T), vec_cols[...])
+    left = jnp.concatenate([vec_rows[...], prod[:, cols:]], 0)
     right = jnp.concatenate([upd_cols, vec_cols[...]], 0)
-    out[...] = matrix[...] - mm(left, right, TN)
+    out[...] = matrix[...] - mm3(left, right, TN)
 
 
 def call(kernel, shapes, *args, scratch=(), cost=None):
@@ -179,13 +198,9 @@
     vec_rows, sent = call(
         product_kernel, [(NB, rows), (n_row, HALF, cols)], rows_t, matrix, inv_s, lower
     )
-    vec_cols, sent = call(
-        reduce_kernel,
-        [(NB, cols), (n_col, HALF, cols + NB)],
-        exchange(sent, "prow"),
-        cols_t,
-        inv_s,
-        lower,
+    (vec_cols,) = call(column_kernel, [(NB, cols)], cols_t, inv_s, lower)
+    (sent,) = call(
+        reduce_kernel, [(n_col, HALF, cols + NB)], exchange(sent, "prow"), vec_cols
     )
     wide = lane_ceil(cols + rows) + NB
     (sent,) = call(spread_kernel, [(n_row, HALF, wide)], exchange(sent, "pcol"))

time: 158 us -> 157 us (level)
  blocking collectives: 130 us -> 110 us
  waiting for transfers between devices: 1.46 us -> 15.7 us
  starting transfers between devices: 3.46 us -> 8.61 us
    all_to_all x6 -> x5, blocking collectives: 130 us -> 110 us  [exchange(): return lax.all_to_all(blocks, axis, 0, 0)]
    all_to_all x1 -> x2, waiting for transfers between devices: 1.46 us -> 15.7 us  [exchange(): return lax.all_to_all(blocks, axis, 0, 0)]
    all_to_all x1 -> x2, starting transfers between devices: 3.46 us -> 8.61 us  [exchange(): return lax.all_to_all(blocks, axis, 0, 0)]
    pallas_call x7 -> x8, Pallas kernels: 21.1 us -> 20.1 us  [call(): pl.pallas_call(kernel, out_shape=outs, scratch_shapes=[pltpu.VMEM(s, jnp....]
  transfers between devices with their start and end apart: 1 -> 2, of which waited for: 1 -> 2; matrix products, arithmetic and copies ran while one was open for 0% -> 0% of each run, Pallas kernels for 9% -> 10%
where the time goes in v4:
time: 157 us; the launch traced here: 156 us
  blocking collectives  110 us (70%)
  Pallas kernels  20.1 us (13%)
  waiting for transfers between devices  15.7 us (10%)
  starting transfers between devices  8.61 us (5%)
    all_to_all x5, blocking collectives, exchange(): return lax.all_to_all(blocks, axis, 0, 0)  110 us
    pallas_call x8, Pallas kernels, call(): pl.pallas_call(kernel, out_shape=outs, scratch_shapes=[pltpu.VMEM(s, jnp....  20.1 us
    all_to_all x2, waiting for transfers between devices, exchange(): return lax.all_to_all(blocks, axis, 0, 0)  15.7 us
    all_to_all x2, starting transfers between devices, exchange(): return lax.all_to_all(blocks, axis, 0, 0)  8.61 us
  transfers between devices with their start and end apart: 2, of which 2 were waited for; matrix products, arithmetic and copies ran while one was open for 0% of the time, Pallas kernels for 10%

profile of v4, /device:TPU:1, one launch (start us, length us, event | category | flops | bytes accessed | tf_op | source)
XLA Modules:
  0.0 156.0 jit_solution(9700190942859406723)
XLA Ops:
  0.6 0.7 broadcast_in_dim.2
  1.4 21.2 %all_to_all.35 = f32[16,8,448]{2,1,0:T(8,128)S(1)} all-to-all(f32[16,8,448]{2,1,0:T(8,128)S(1)} %broadcast_in_dim.2), channel_id=1, replica_groups=mesh['prow'=32,'pcol'=16] {'pcol'}, dimensions={0} | all-to-all | bytes 458752 | tf_op jit(solution)/shard_map/all_to_all | solution.py:178
  22.5 0.4 shard_map.41
  22.9 30.7 %all_to_all.36.got = f32[32,8,576]{2,1,0:T(8,128)S(1)} all-to-all(f32[32,8,576]{2,1,0:T(8,128)S(1)} %shard_map.41), channel_id=1, replica_groups=mesh['prow'=32,'pcol'=16] {'prow'}, dimensions={0} | all-to-all | bytes 1179648 | tf_op jit(solution)/shard_map/all_to_all | solution.py:178
  53.6 0.9 shard_map.42
  54.5 13.4 %all_to_all.37.got = f32[16,8,256]{2,1,0:T(8,128)S(1)} all-to-all(f32[16,8,256]{2,1,0:T(8,128)S(1)} %get-tuple-element.10), channel_id=1, replica_groups=mesh['prow'=32,'pcol'=16] {'pcol'}, dimensions={0} | all-to-all | bytes 262144 | tf_op jit(solution)/shard_map/all_to_all | solution.py:178
  67.9 3.5 %all-to-all-start.3 = ((f32[16,8,896]{2,1,0:T(8,128)}), f32[16,8,896]{2,1,0:T(8,128)S(1)}, u32[]{:S(2)}, u32[]{:S(2)}) async-start(f32[16,8,896]{2,1,0:T(8,128)} %get-tuple-element.14), calls=%async_computation.3 | async-start | bytes 917504 | tf_op jit(solution)/shard_map/all_to_all | solution.py:178
  71.4 0.0 copy-start
  71.4 12.7 %shard_map.43 = (f32[128,128]{1,0:T(8,128)}, f32[128,128]{1,0:T(8,128)S(1)}, f32[128,128]{1,0:T(8,128)S(1)}, f32[128,128]{1,0:T(8,128)S(1)}) custom-call(f32[16,8,256]{2,1,0:T(8,128)S(1)} %all_to_all.37.got), custom_call_target="tpu_custom_call" | custom-call | flops 20000000000 | bytes 1048576 | tf_op jit(solution)/shard_map/pallas_call | solution.py:168
  84.0 0.0 copy-done
  84.0 2.2 %shard_map.44 = (f32[128,448]{1,0:T(8,128)S(1)}, f32[32,4,896]{2,1,0:T(4,128)}) custom-call(f32[128,448]{1,0:T(8,128)S(1)} %bitcast.4, f32[448,896]{1,0:T(8,128)S(1)} %copy-done, f32[128,128]{1,0:T(8,128)S(1)} %get-tuple-element.11.inv_s, f32[128,128]{1,0:T(8,128)S(1)} %get-tuple-element.12.lower), custom_call_target="tpu_custom_call" | custom-call | tf_op jit(solution)/shard_map/pallas_call | solution.py:168
  86.2 0.7 all-to-all-done.3
  86.9 5.1 %all-to-all-start.4 = ((f32[32,4,896]{2,1,0:T(4,128)}), f32[32,4,896]{2,1,0:T(4,128)S(1)}, u32[]{:S(2)}, u32[]{:S(2)}) async-start(f32[32,4,896]{2,1,0:T(4,128)} %get-tuple-element.15), calls=%async_computation.4 | async-start | bytes 917504 | tf_op jit(solution)/shard_map/all_to_all | solution.py:178
  92.1 0.6 shard_map.45.vec_cols
  92.6 15.0 %all-to-all-done.4.got = f32[32,4,896]{2,1,0:T(4,128)S(1)} async-done(((f32[32,4,896]{2,1,0:T(4,128)}), f32[32,4,896]{2,1,0:T(4,128)S(1)}, u32[]{:S(2)}, u32[]{:S(2)}) %all-to-all-start.4) | async-done | bytes 458784 | tf_op jit(solution)/shard_map/all_to_all | solution.py:178
  107.6 0.4 shard_map.46
  108.0 18.0 %all_to_all.38.got = f32[16,4,1024]{2,1,0:T(4,128)S(1)} all-to-all(f32[16,4,1024]{2,1,0:T(4,128)S(1)} %shard_map.46), channel_id=1, replica_groups=mesh['prow'=32,'pcol'=16] {'pcol'}, dimensions={0} | all-to-all | bytes 524288 | tf_op jit(solution)/shard_map/all_to_all | solution.py:178
  126.0 0.1 shard_map.47
  126.1 26.9 %all_to_all.39.got = f32[32,4,1536]{2,1,0:T(4,128)S(1)} all-to-all(f32[32,4,1536]{2,1,0:T(4,128)S(1)} %shard_map.47), channel_id=1, replica_groups=mesh['prow'=32,'pcol'=16] {'prow'}, dimensions={0} | all-to-all | bytes 1572864 | tf_op jit(solution)/shard_map/all_to_all | solution.py:178
  153.0 3.0 %shard_map.48 = f32[448,896]{1,0:T(8,128)} custom-call(f32[128,448]{1,0:T(8,128)S(1)} %get-tuple-element.13.vec_rows, f32[128,896]{1,0:T(8,128)S(1)} %shard_map.45.vec_cols, f32[32,4,1536]{2,1,0:T(4,128)S(1)} %all_to_all.39.got, f32[448,896]{1,0:T(8,128)S(1)} %copy-done, f32[128,128]{1,0:T(8,128)S(1)} %get-tuple-element.16.tfac), custom_call_target="tpu_custom_call" | custom-call | tf_op jit(solution)/shard_map/pallas_call | solution.py:168
Async XLA Ops:
  67.9 19.0 %all-to-all-start.3 = ((f32[16,8,896]{2,1,0:T(8,128)}), f32[16,8,896]{2,1,0:T(8,128)S(1)}, u32[]{:S(2)}, u32[]{:S(2)}) async-start(f32[16,8,896]{2,1,0:T(8,128)} %get-tuple-element.14), calls=%async_computation.3 | async-start | bytes 917504 | tf_op jit(solution)/shard_map/all_to_all | solution.py:178
  71.4 12.7 %copy-start = (f32[448,896]{1,0:T(8,128)S(1)}, f32[448,896]{1,0:T(8,128)}, u32[]{:S(2)}) copy-start(f32[448,896]{1,0:T(8,128)} %matrix.3) | copy-start | bytes 4816900
  86.9 20.7 %all-to-all-start.4 = ((f32[32,4,896]{2,1,0:T(4,128)}), f32[32,4,896]{2,1,0:T(4,128)S(1)}, u32[]{:S(2)}, u32[]{:S(2)}) async-start(f32[32,4,896]{2,1,0:T(4,128)} %get-tuple-element.15), calls=%async_computation.4 | async-start | bytes 917504 | tf_op jit(solution)/shard_map/all_to_all | solution.py:178

commit v5 on v4

--- a/solution.py
+++ b/solution.py
@@ -47,22 +47,34 @@
 
 
 def gram_kernel(rows_t, sent):
-    own = pl.ds(pl.multiple_of(lax.axis_index("pcol") * SUB, SUB), SUB)
+    j = lax.axis_index("pcol")
+    own = pl.ds(pl.multiple_of(j * SUB, SUB), SUB)
     block = rows_t[own, :]
     gram = mm(block, rows_t[...], NT)
+    first = rows_t[:SUB, :NB]
+    extra = jnp.where(j == 1, first[:HALF], first[HALF:])
+    pad = jnp.zeros((HALF, rows_t.shape[1] - 3 * NB), jnp.float32)
+    top = jnp.concatenate([block[:HALF, :NB], block[HALF:, :NB], extra, pad], 1)
+    use_top = (lax.axis_index("prow") == 0) & (j > 0)
     for dest in range(sent.shape[0]):
-        sent[dest, :, :NB] = gram
-        sent[dest, :, NB:] = block
+        sent[dest, :, :NB] = gram[:HALF]
+        sent[dest, :, NB : 2 * NB] = gram[HALF:]
+        piece = rows_t[dest * HALF : (dest + 1) * HALF, :]
+        sent[dest, :, 2 * NB :] = jnp.where(use_top, top, piece)
 
 
 def sort_kernel(got, small, blocks):
-    rows = got.shape[2] - NB
-    gram = jnp.sum(got[:, :, :NB], axis=0)
+    j = lax.axis_index("pcol")
+    gram = jnp.sum(got[:, :, : 2 * NB], axis=0)
+    top = got[0, :, 2 * NB : 5 * NB]
+    left = got[2 * j, :, 2 * NB :]
+    right = got[2 * j + 1, :, 2 * NB :]
+    both = jnp.concatenate([left, right], 1)
     for dest in range(small.shape[0]):
-        small[dest, :, :NB] = gram
-        small[dest, :, NB:] = got[0, :, NB : 2 * NB]
-        blocks[dest, :, :rows] = got[2 * dest, :, NB:]
-        blocks[dest, :, rows:] = got[2 * dest + 1, :, NB:]
+        small[dest, :, : 2 * NB] = gram
+        small[dest, :, 2 * NB :] = top
+    for dest in range(blocks.shape[0]):
+        blocks[dest] = both
 
 
 def vectors(panel_t, combine, low, is_first):
@@ -79,7 +91,9 @@
         sent[dest] = part[dest * HALF : (dest + 1) * HALF]
 
 
-def column_kernel(cols_t, inv_s, lower, vec_cols):
+def column_kernel(got, inv_s, lower, vec_cols, cols_t):
+    for part in range(got.shape[0]):
+        cols_t[part * HALF : (part + 1) * HALF, :] = got[part]
     vec_cols[...] = vectors(
         cols_t[...], -inv_s[...], lower[...], lax.axis_index("pcol") == 0
     )
@@ -116,8 +130,11 @@
     lane = lax.broadcasted_iota(jnp.int32, (1, NB), 1)
     eye = jnp.where(rows == lanes, 1.0, 0.0)
     for part in range(got.shape[0]):
-        work[part * SUB : (part + 1) * SUB, :] = got[part, :, :NB]
-        rest[part * SUB : (part + 1) * SUB, :] = -got[part, :, NB:]
+        for half in range(2):
+            to = slice(part * SUB + half * HALF, part * SUB + (half + 1) * HALF)
+            work[to, :] = got[part, :, half * NB : (half + 1) * NB]
+            source, at = (half + 1, 4) if part == 0 else (part, 2 + half)
+            rest[to, :] = -got[source, :, at * NB : (at + 1) * NB]
     rest[...] = rest[...].T
     inv_c[...] = eye
     inv_l[...] = eye
@@ -183,9 +200,9 @@
     n_row, n_col = lax.axis_size("prow"), lax.axis_size("pcol")
     block_t = jnp.broadcast_to(panel.T[None], (n_col, SUB, rows))
     rows_t = exchange(block_t, "pcol").reshape(NB, rows)
-    (sent,) = call(gram_kernel, [(n_row, SUB, NB + rows)], rows_t)
+    (sent,) = call(gram_kernel, [(n_row, HALF, 2 * NB + rows)], rows_t)
     small, blocks = call(
-        sort_kernel, [(n_col, SUB, 2 * NB), (n_col, SUB, cols)], exchange(sent, "prow")
+        sort_kernel, [(n_col, HALF, 5 * NB), (n_row, HALF, cols)], exchange(sent, "prow")
     )
     band, inv_s, lower, tfac = call(
         factor_kernel,
@@ -194,11 +211,13 @@
         scratch=[(NB, NB)] * 5,
         cost=pl.CostEstimate(flops=2 * 10**10, bytes_accessed=2**20, transcendentals=0),
     )
-    cols_t = exchange(blocks, "pcol").reshape(NB, cols)
+    cols_t = exchange(blocks, "prow")
     vec_rows, sent = call(
         product_kernel, [(NB, rows), (n_row, HALF, cols)], rows_t, matrix, inv_s, lower
     )
-    (vec_cols,) = call(column_kernel, [(NB, cols)], cols_t, inv_s, lower)
+    (vec_cols,) = call(
+        column_kernel, [(NB, cols)], cols_t, inv_s, lower, scratch=[(NB, cols)]
+    )
     (sent,) = call(
         reduce_kernel, [(n_col, HALF, cols + NB)], exchange(sent, "prow"), vec_cols
     )

time: 157 us -> 154 us (0.981)
  starting transfers between devices: 8.61 us -> 14.1 us
  blocking collectives: 110 us -> 105 us
  waiting for transfers between devices: 15.7 us -> 13.2 us
    all_to_all x5, blocking collectives: 110 us -> 105 us  [exchange(): return lax.all_to_all(blocks, axis, 0, 0)]
    all_to_all x2, starting transfers between devices: 8.61 us -> 14.1 us  [exchange(): return lax.all_to_all(blocks, axis, 0, 0)]
    all_to_all x2, waiting for transfers between devices: 15.7 us -> 13.2 us  [exchange(): return lax.all_to_all(blocks, axis, 0, 0)]
where the time goes in v5:
time: 154 us; the launch traced here: 153 us
  blocking collectives  105 us (68%)
  Pallas kernels  20.1 us (13%)
  starting transfers between devices  14.1 us (9%)
  waiting for transfers between devices  13.2 us (9%)
    all_to_all x5, blocking collectives, exchange(): return lax.all_to_all(blocks, axis, 0, 0)  105 us
    pallas_call x8, Pallas kernels, call(): pl.pallas_call(kernel, out_shape=outs, scratch_shapes=[pltpu.VMEM(s, jnp....  20.1 us
    all_to_all x2, starting transfers between devices, exchange(): return lax.all_to_all(blocks, axis, 0, 0)  14.1 us
    all_to_all x2, waiting for transfers between devices, exchange(): return lax.all_to_all(blocks, axis, 0, 0)  13.2 us
  transfers between devices with their start and end apart: 2, of which 2 were waited for; matrix products, arithmetic and copies ran while one was open for 0% of the time, Pallas kernels for 10%

profile of v5, /device:TPU:1, one launch (start us, length us, event | category | flops | bytes accessed | tf_op | source)
XLA Modules:
  0.0 153.4 jit_solution(11458677992797621614)
XLA Ops:
  0.6 0.7 broadcast_in_dim.2
  1.4 21.2 %all_to_all.35 = f32[16,8,448]{2,1,0:T(8,128)S(1)} all-to-all(f32[16,8,448]{2,1,0:T(8,128)S(1)} %broadcast_in_dim.2), channel_id=1, replica_groups=mesh['prow'=32,'pcol'=16] {'pcol'}, dimensions={0} | all-to-all | bytes 458752 | tf_op jit(solution)/shard_map/all_to_all | solution.py:195
  22.5 0.4 shard_map.41
  22.9 25.0 %all_to_all.36.got = f32[32,4,704]{2,1,0:T(4,128)S(1)} all-to-all(f32[32,4,704]{2,1,0:T(4,128)S(1)} %shard_map.41), channel_id=1, replica_groups=mesh['prow'=32,'pcol'=16] {'prow'}, dimensions={0} | all-to-all | bytes 720896 | tf_op jit(solution)/shard_map/all_to_all | solution.py:195
  47.9 0.9 shard_map.42
  48.7 14.2 %all_to_all.37.got = f32[16,4,640]{2,1,0:T(4,128)S(1)} all-to-all(f32[16,4,640]{2,1,0:T(4,128)S(1)} %get-tuple-element.10), channel_id=1, replica_groups=mesh['prow'=32,'pcol'=16] {'pcol'}, dimensions={0} | all-to-all | bytes 327680 | tf_op jit(solution)/shard_map/all_to_all | solution.py:195
  62.9 5.1 %all-to-all-start.3 = ((f32[32,4,896]{2,1,0:T(4,128)}), f32[32,4,896]{2,1,0:T(4,128)S(1)}, u32[]{:S(2)}, u32[]{:S(2)}) async-start(f32[32,4,896]{2,1,0:T(4,128)} %get-tuple-element.14), calls=%async_computation.3 | async-start | bytes 917504 | tf_op jit(solution)/shard_map/all_to_all | solution.py:195
  68.1 0.0 copy-start
  68.1 12.7 %shard_map.43 = (f32[128,128]{1,0:T(8,128)}, f32[128,128]{1,0:T(8,128)S(1)}, f32[128,128]{1,0:T(8,128)S(1)}, f32[128,128]{1,0:T(8,128)S(1)}) custom-call(f32[16,4,640]{2,1,0:T(4,128)S(1)} %all_to_all.37.got), custom_call_target="tpu_custom_call" | custom-call | flops 20000000000 | bytes 1048576 | tf_op jit(solution)/shard_map/pallas_call | solution.py:185
  80.7 0.0 copy-done
  80.8 2.2 %shard_map.44 = (f32[128,448]{1,0:T(8,128)S(1)}, f32[32,4,896]{2,1,0:T(4,128)}) custom-call(f32[128,448]{1,0:T(8,128)S(1)} %bitcast.3, f32[448,896]{1,0:T(8,128)S(1)} %copy-done, f32[128,128]{1,0:T(8,128)S(1)} %get-tuple-element.11.inv_s, f32[128,128]{1,0:T(8,128)S(1)} %get-tuple-element.12.lower), custom_call_target="tpu_custom_call" | custom-call | tf_op jit(solution)/shard_map/pallas_call | solution.py:185
  82.9 0.4 all-to-all-done.3.got
  83.3 9.0 %all-to-all-start.4 = ((f32[32,4,896]{2,1,0:T(4,128)}), f32[32,4,896]{2,1,0:T(4,128)S(1)}, u32[]{:S(2)}, u32[]{:S(2)}) async-start(f32[32,4,896]{2,1,0:T(4,128)} %get-tuple-element.15), calls=%async_computation.4 | async-start | bytes 917504 | tf_op jit(solution)/shard_map/all_to_all | solution.py:195
  92.3 0.6 shard_map.45.vec_cols
  92.9 12.8 %all-to-all-done.4.got = f32[32,4,896]{2,1,0:T(4,128)S(1)} async-done(((f32[32,4,896]{2,1,0:T(4,128)}), f32[32,4,896]{2,1,0:T(4,128)S(1)}, u32[]{:S(2)}, u32[]{:S(2)}) %all-to-all-start.4) | async-done | bytes 458784 | tf_op jit(solution)/shard_map/all_to_all | solution.py:195
  105.7 0.4 shard_map.46
  106.1 17.1 %all_to_all.38.got = f32[16,4,1024]{2,1,0:T(4,128)S(1)} all-to-all(f32[16,4,1024]{2,1,0:T(4,128)S(1)} %shard_map.46), channel_id=1, replica_groups=mesh['prow'=32,'pcol'=16] {'pcol'}, dimensions={0} | all-to-all | bytes 524288 | tf_op jit(solution)/shard_map/all_to_all | solution.py:195
  123.2 0.1 shard_map.47
  123.3 27.1 %all_to_all.39.got = f32[32,4,1536]{2,1,0:T(4,128)S(1)} all-to-all(f32[32,4,1536]{2,1,0:T(4,128)S(1)} %shard_map.47), channel_id=1, replica_groups=mesh['prow'=32,'pcol'=16] {'prow'}, dimensions={0} | all-to-all | bytes 1572864 | tf_op jit(solution)/shard_map/all_to_all | solution.py:195
  150.5 3.0 %shard_map.48 = f32[448,896]{1,0:T(8,128)} custom-call(f32[128,448]{1,0:T(8,128)S(1)} %get-tuple-element.13.vec_rows, f32[128,896]{1,0:T(8,128)S(1)} %shard_map.45.vec_cols, f32[32,4,1536]{2,1,0:T(4,128)S(1)} %all_to_all.39.got, f32[448,896]{1,0:T(8,128)S(1)} %copy-done, f32[128,128]{1,0:T(8,128)S(1)} %get-tuple-element.16.tfac), custom_call_target="tpu_custom_call" | custom-call | tf_op jit(solution)/shard_map/pallas_call | solution.py:185
Async XLA Ops:
  62.9 20.4 %all-to-all-start.3 = ((f32[32,4,896]{2,1,0:T(4,128)}), f32[32,4,896]{2,1,0:T(4,128)S(1)}, u32[]{:S(2)}, u32[]{:S(2)}) async-start(f32[32,4,896]{2,1,0:T(4,128)} %get-tuple-element.14), calls=%async_computation.3 | async-start | bytes 917504 | tf_op jit(solution)/shard_map/all_to_all | solution.py:195
  68.1 12.7 %copy-start = (f32[448,896]{1,0:T(8,128)S(1)}, f32[448,896]{1,0:T(8,128)}, u32[]{:S(2)}) copy-start(f32[448,896]{1,0:T(8,128)} %matrix.3) | copy-start | bytes 4816900
  83.3 22.4 %all-to-all-start.4 = ((f32[32,4,896]{2,1,0:T(4,128)}), f32[32,4,896]{2,1,0:T(4,128)S(1)}, u32[]{:S(2)}, u32[]{:S(2)}) async-start(f32[32,4,896]{2,1,0:T(4,128)} %get-tuple-element.15), calls=%async_computation.4 | async-start | bytes 917504 | tf_op jit(solution)/shard_map/all_to_all | solution.py:195

commit v6 on v5

--- a/solution.py
+++ b/solution.py
@@ -6,10 +6,11 @@
 from jax.sharding import PartitionSpec as P
 
 PRECISE = lax.Precision.HIGHEST
-VMEM_BYTES = 48 * 2**20
+VMEM_BYTES = 24 * 2**20
 NB = 128
 SUB = 8
 HALF = SUB // 2
+STEP = 4
 
 
 def mm(left, right, contract=((1,), (0,))):
@@ -136,33 +137,70 @@
             source, at = (half + 1, 4) if part == 0 else (part, 2 + half)
             rest[to, :] = -got[source, :, at * NB : (at + 1) * NB]
     rest[...] = rest[...].T
-    inv_c[...] = eye
-    inv_l[...] = eye
-    inv_s[...] = eye
-    scales = jnp.zeros((1, NB), jnp.float32)
-    for k in range(NB):
-        lo = (k // SUB) * SUB
+    for ref in (inv_c, inv_l, inv_s, lower):
+        ref[...] = eye
+
+    def spread(column):
+        return jnp.broadcast_to(column, (column.shape[0], NB))
+
+    for first in range(0, NB, STEP):
+        lo = first // SUB * SUB
         hi = lo + SUB
-        below = rows[lo:, :1] > k
-        inv = lax.rsqrt(work[k : k + 1, k : k + 1])
-        c_row = jnp.where(lane >= k, work[k : k + 1, :] * inv, 0.0)
-        band[k : k + 1, :] = -c_row
-        c_col = jnp.where(below, work[lo:, k : k + 1] * inv, 0.0)
-        x_row = inv_c[k : k + 1, :] * inv
-        s_row = jnp.where(lane >= k, rest[k : k + 1, :] - c_row, 0.0)
-        scale = 1.0 / (rest[k : k + 1, k : k + 1] - c_row[:, k : k + 1])
-        l_col = jnp.where(below, rest[lo:, k : k + 1] * scale, 0.0)
-        l_row = inv_l[k : k + 1, :]
-        right = jnp.where(lane > k, s_row, 0.0)
-        upper[k : k + 1, :] = s_row
-        scales = jnp.where(lane == k, scale, scales)
-        work[lo:, :] = work[lo:, :] - c_col * c_row
-        inv_c[lo:, :] = jnp.where(rows[lo:] == k, x_row, inv_c[lo:, :] - c_col * x_row)
-        rest[lo:, :] = rest[lo:, :] - l_col * right
-        inv_l[lo:, :] = inv_l[lo:, :] - l_col * l_row
-        s_col = inv_s[:hi, k : k + 1] * scale
-        inv_s[:hi, :] = jnp.where(lanes[:hi] == k, s_col, inv_s[:hi, :] - s_col * right)
-    lower[...] = jnp.where(rows > lanes, rest[...] * scales, eye)
+        block = range(first, first + STEP)
+        row_at = rows[lo:]
+        gram_col = [spread(work[lo:, k : k + 1]) for k in block]
+        rest_col = [spread(rest[lo:, k : k + 1]) for k in block]
+        inv_col = [spread(inv_s[:hi, k : k + 1]) for k in block]
+        gram_row = [work[k : k + 1, :] for k in block]
+        rest_row = [rest[k : k + 1, :] for k in block]
+        c_inv_row = [inv_c[k : k + 1, :] for k in block]
+        l_inv_row = [inv_l[k : k + 1, :] for k in block]
+        done = []
+        for t, k in enumerate(block):
+            here = slice(k - lo, k - lo + 1)
+            pivot = gram_col[t][here]
+            inv = lax.rsqrt(pivot)
+            c_col = jnp.where(row_at > k, gram_col[t] * inv, 0.0)
+            c_row = jnp.where(lane >= k, gram_row[t] * inv, 0.0)
+            x_row = c_inv_row[t] * inv
+            s_row = jnp.where(lane >= k, rest_row[t] - c_row, 0.0)
+            scale = 1.0 / (rest_col[t][here] - pivot * inv)
+            l_col = jnp.where(row_at > k, rest_col[t] * scale, 0.0)
+            right = jnp.where(lane > k, s_row, 0.0)
+            x_col = inv_col[t] * scale
+            l_row = l_inv_row[t]
+            band[k : k + 1, :] = -c_row
+            upper[k : k + 1, :] = s_row
+            for u in range(t + 1, STEP):
+                there = slice(first + u - lo, first + u - lo + 1)
+                c, l = c_col[there], l_col[there]
+                s = rest_col[u][here] - c
+                gram_col[u] = gram_col[u] - c_col * c
+                rest_col[u] = rest_col[u] - l_col * s
+                inv_col[u] = inv_col[u] - x_col * s
+                gram_row[u] = gram_row[u] - c * c_row
+                c_inv_row[u] = c_inv_row[u] - c * x_row
+                rest_row[u] = rest_row[u] - l * right
+                l_inv_row[u] = l_inv_row[u] - l * l_row
+            done.append((c_col, c_row, x_row, l_col, l_row, right, x_col))
+        below = (first + STEP) // SUB * SUB
+        if below < NB:
+            for ref, col, row in ((work, 0, 1), (rest, 3, 5), (inv_c, 0, 2), (inv_l, 3, 4)):
+                total = ref[below:, :]
+                for terms in done:
+                    total = total - terms[col][below - lo :] * terms[row]
+                ref[below:, :] = total
+        above = inv_s[:hi, :]
+        for terms in done:
+            above = above - terms[6] * terms[5]
+        low = lower[lo:, :]
+        for k, terms in zip(block, done):
+            above = jnp.where(lanes[:hi] == k, terms[6], above)
+            low = jnp.where((lanes[lo:] == k) & (row_at > k), terms[3], low)
+            inv_c[k : k + 1, :] = terms[2]
+            inv_l[k : k + 1, :] = terms[4]
+        inv_s[:hi, :] = above
+        lower[lo:, :] = low
     tfac[...] = -mm(upper[...], mm(inv_l[...], inv_c[...]), NT)
 
 
@@ -180,13 +218,13 @@
     out[...] = matrix[...] - mm3(left, right, TN)
 
 
-def call(kernel, shapes, *args, scratch=(), cost=None):
+def call(kernel, shapes, *args, scratch=(), cost=None, vmem=VMEM_BYTES):
     outs = [jax.ShapeDtypeStruct(s, jnp.float32) for s in shapes]
     return pl.pallas_call(
         kernel,
         out_shape=outs,
         scratch_shapes=[pltpu.VMEM(s, jnp.float32) for s in scratch],
-        compiler_params=pltpu.CompilerParams(vmem_limit_bytes=VMEM_BYTES),
+        compiler_params=pltpu.CompilerParams(vmem_limit_bytes=vmem),
         cost_estimate=cost,
     )(*args)
 
@@ -210,6 +248,7 @@
         exchange(small, "pcol"),
         scratch=[(NB, NB)] * 5,
         cost=pl.CostEstimate(flops=2 * 10**10, bytes_accessed=2**20, transcendentals=0),
+        vmem=8 * 2**20,
     )
     cols_t = exchange(blocks, "prow")
     vec_rows, sent = call(

time: 154 us -> 151 us (0.981)
  Pallas kernels: 20.1 us -> 14.2 us
  waiting for transfers between devices: 13.2 us -> 18.7 us
  starting transfers between devices: 14.1 us -> 11 us
    pallas_call x8, Pallas kernels: 20.1 us -> 14.2 us  [call(): pl.pallas_call(kernel, out_shape=outs, scratch_shapes=[pltpu.VMEM(s, jnp....]
    all_to_all x2, waiting for transfers between devices: 13.2 us -> 18.7 us  [exchange(): return lax.all_to_all(blocks, axis, 0, 0)]
    all_to_all x2, starting transfers between devices: 14.1 us -> 11 us  [exchange(): return lax.all_to_all(blocks, axis, 0, 0)]
  transfers between devices with their start and end apart: 2 -> 2, of which waited for: 2 -> 2; matrix products, arithmetic and copies ran while one was open for 0% -> 0% of each run, Pallas kernels for 10% -> 6%
where the time goes in v6:
time: 151 us
  blocking collectives  105 us (70%)
  waiting for transfers between devices  18.7 us (12%)
  Pallas kernels  14.2 us (9%)
  starting transfers between devices  11 us (7%)
    all_to_all x5, blocking collectives, exchange(): return lax.all_to_all(blocks, axis, 0, 0)  105 us
    all_to_all x2, waiting for transfers between devices, exchange(): return lax.all_to_all(blocks, axis, 0, 0)  18.7 us
    pallas_call x8, Pallas kernels, call(): pl.pallas_call(kernel, out_shape=outs, scratch_shapes=[pltpu.VMEM(s, jnp....  14.2 us
    all_to_all x2, starting transfers between devices, exchange(): return lax.all_to_all(blocks, axis, 0, 0)  11 us
  transfers between devices with their start and end apart: 2, of which 2 were waited for; matrix products, arithmetic and copies ran while one was open for 0% of the time, Pallas kernels for 6%

profile of v6, /device:TPU:1, one launch (start us, length us, event | category | flops | bytes accessed | tf_op | source)
XLA Modules:
  0.0 150.6 jit_solution(9105631895750937254)
XLA Ops:
  0.6 0.7 broadcast_in_dim.2
  1.4 21.2 %all_to_all.35 = f32[16,8,448]{2,1,0:T(8,128)S(1)} all-to-all(f32[16,8,448]{2,1,0:T(8,128)S(1)} %broadcast_in_dim.2), channel_id=1, replica_groups=mesh['prow'=32,'pcol'=16] {'pcol'}, dimensions={0} | all-to-all | bytes 458752 | tf_op jit(solution)/shard_map/all_to_all | solution.py:233
  22.5 0.4 shard_map.41
  22.9 25.0 %all_to_all.36.got = f32[32,4,704]{2,1,0:T(4,128)S(1)} all-to-all(f32[32,4,704]{2,1,0:T(4,128)S(1)} %shard_map.41), channel_id=1, replica_groups=mesh['prow'=32,'pcol'=16] {'prow'}, dimensions={0} | all-to-all | bytes 720896 | tf_op jit(solution)/shard_map/all_to_all | solution.py:233
  47.9 0.9 shard_map.42
  48.7 14.2 %all_to_all.37.got = f32[16,4,640]{2,1,0:T(4,128)S(1)} all-to-all(f32[16,4,640]{2,1,0:T(4,128)S(1)} %get-tuple-element.10), channel_id=1, replica_groups=mesh['prow'=32,'pcol'=16] {'pcol'}, dimensions={0} | all-to-all | bytes 327680 | tf_op jit(solution)/shard_map/all_to_all | solution.py:233
  62.9 5.1 %all-to-all-start.3 = ((f32[32,4,896]{2,1,0:T(4,128)}), f32[32,4,896]{2,1,0:T(4,128)S(1)}, u32[]{:S(2)}, u32[]{:S(2)}) async-start(f32[32,4,896]{2,1,0:T(4,128)} %get-tuple-element.14), calls=%async_computation.3 | async-start | bytes 917504 | tf_op jit(solution)/shard_map/all_to_all | solution.py:233
  68.1 0.0 copy-start
  68.1 6.8 %shard_map.43 = (f32[128,128]{1,0:T(8,128)}, f32[128,128]{1,0:T(8,128)S(1)}, f32[128,128]{1,0:T(8,128)S(1)}, f32[128,128]{1,0:T(8,128)S(1)}) custom-call(f32[16,4,640]{2,1,0:T(4,128)S(1)} %all_to_all.37.got), custom_call_target="tpu_custom_call" | custom-call | flops 20000000000 | bytes 1048576 | tf_op jit(solution)/shard_map/pallas_call | solution.py:223
  74.8 0.0 copy-done
  74.8 2.2 %shard_map.44 = (f32[128,448]{1,0:T(8,128)S(1)}, f32[32,4,896]{2,1,0:T(4,128)}) custom-call(f32[128,448]{1,0:T(8,128)S(1)} %bitcast.3, f32[448,896]{1,0:T(8,128)S(1)} %copy-done, f32[128,128]{1,0:T(8,128)S(1)} %get-tuple-element.11.inv_s, f32[128,128]{1,0:T(8,128)S(1)} %get-tuple-element.12.lower), custom_call_target="tpu_custom_call" | custom-call | tf_op jit(solution)/shard_map/pallas_call | solution.py:223
  77.0 6.4 %all-to-all-done.3.got = f32[32,4,896]{2,1,0:T(4,128)S(1)} async-done(((f32[32,4,896]{2,1,0:T(4,128)}), f32[32,4,896]{2,1,0:T(4,128)S(1)}, u32[]{:S(2)}, u32[]{:S(2)}) %all-to-all-start.3) | async-done | bytes 458784 | tf_op jit(solution)/shard_map/all_to_all | solution.py:233
  83.3 5.9 %all-to-all-start.4 = ((f32[32,4,896]{2,1,0:T(4,128)}), f32[32,4,896]{2,1,0:T(4,128)S(1)}, u32[]{:S(2)}, u32[]{:S(2)}) async-start(f32[32,4,896]{2,1,0:T(4,128)} %get-tuple-element.15), calls=%async_computation.4 | async-start | bytes 917504 | tf_op jit(solution)/shard_map/all_to_all | solution.py:233
  89.3 0.6 shard_map.45.vec_cols
  89.9 12.4 %all-to-all-done.4.got = f32[32,4,896]{2,1,0:T(4,128)S(1)} async-done(((f32[32,4,896]{2,1,0:T(4,128)}), f32[32,4,896]{2,1,0:T(4,128)S(1)}, u32[]{:S(2)}, u32[]{:S(2)}) %all-to-all-start.4) | async-done | bytes 458784 | tf_op jit(solution)/shard_map/all_to_all | solution.py:233
  102.2 0.4 shard_map.46
  102.6 17.6 %all_to_all.38.got = f32[16,4,1024]{2,1,0:T(4,128)S(1)} all-to-all(f32[16,4,1024]{2,1,0:T(4,128)S(1)} %shard_map.46), channel_id=1, replica_groups=mesh['prow'=32,'pcol'=16] {'pcol'}, dimensions={0} | all-to-all | bytes 524288 | tf_op jit(solution)/shard_map/all_to_all | solution.py:233
  120.1 0.1 shard_map.47
  120.3 27.3 %all_to_all.39.got = f32[32,4,1536]{2,1,0:T(4,128)S(1)} all-to-all(f32[32,4,1536]{2,1,0:T(4,128)S(1)} %shard_map.47), channel_id=1, replica_groups=mesh['prow'=32,'pcol'=16] {'prow'}, dimensions={0} | all-to-all | bytes 1572864 | tf_op jit(solution)/shard_map/all_to_all | solution.py:233
  147.6 3.0 %shard_map.48 = f32[448,896]{1,0:T(8,128)} custom-call(f32[128,448]{1,0:T(8,128)S(1)} %get-tuple-element.13.vec_rows, f32[128,896]{1,0:T(8,128)S(1)} %shard_map.45.vec_cols, f32[32,4,1536]{2,1,0:T(4,128)S(1)} %all_to_all.39.got, f32[448,896]{1,0:T(8,128)S(1)} %copy-done, f32[128,128]{1,0:T(8,128)S(1)} %get-tuple-element.16.tfac), custom_call_target="tpu_custom_call" | custom-call | tf_op jit(solution)/shard_map/pallas_call | solution.py:223
Async XLA Ops:
  62.9 20.4 %all-to-all-start.3 = ((f32[32,4,896]{2,1,0:T(4,128)}), f32[32,4,896]{2,1,0:T(4,128)S(1)}, u32[]{:S(2)}, u32[]{:S(2)}) async-start(f32[32,4,896]{2,1,0:T(4,128)} %get-tuple-element.14), calls=%async_computation.3 | async-start | bytes 917504 | tf_op jit(solution)/shard_map/all_to_all | solution.py:233
  68.1 6.8 %copy-start = (f32[448,896]{1,0:T(8,128)S(1)}, f32[448,896]{1,0:T(8,128)}, u32[]{:S(2)}) copy-start(f32[448,896]{1,0:T(8,128)} %matrix.3) | copy-start | bytes 4816900
  83.3 18.9 %all-to-all-start.4 = ((f32[32,4,896]{2,1,0:T(4,128)}), f32[32,4,896]{2,1,0:T(4,128)S(1)}, u32[]{:S(2)}, u32[]{:S(2)}) async-start(f32[32,4,896]{2,1,0:T(4,128)} %get-tuple-element.15), calls=%async_computation.4 | async-start | bytes 917504 | tf_op jit(solution)/shard_map/all_to_all | solution.py:233

commit v7 on v6

--- a/solution.py
+++ b/solution.py
@@ -74,8 +74,7 @@
     for dest in range(small.shape[0]):
         small[dest, :, : 2 * NB] = gram
         small[dest, :, 2 * NB :] = top
-    for dest in range(blocks.shape[0]):
-        blocks[dest] = both
+    blocks[...] = both
 
 
 def vectors(panel_t, combine, low, is_first):
@@ -84,26 +83,24 @@
     return jnp.concatenate([head, vec[:, NB:]], 1)
 
 
-def product_kernel(rows_t, matrix, inv_s, lower, vec_rows, sent):
+def product_kernel(rows_t, blocks, matrix, inv_s, lower, vec_rows, sent):
     vec = vectors(rows_t[...], -inv_s[...], lower[...], lax.axis_index("prow") == 0)
     vec_rows[...] = vec
     part = mm(vec, matrix[...])
+    block = blocks[...]
     for dest in range(sent.shape[0]):
-        sent[dest] = part[dest * HALF : (dest + 1) * HALF]
-
-
-def column_kernel(got, inv_s, lower, vec_cols, cols_t):
-    for part in range(got.shape[0]):
-        cols_t[part * HALF : (part + 1) * HALF, :] = got[part]
-    vec_cols[...] = vectors(
-        cols_t[...], -inv_s[...], lower[...], lax.axis_index("pcol") == 0
-    )
-
-
-def reduce_kernel(got, vec_cols, sent):
+        sent[dest, :HALF, :] = part[dest * HALF : (dest + 1) * HALF]
+        sent[dest, HALF:, :] = block
+
+
+def reduce_kernel(got, inv_s, lower, vec_cols, sent, cols_t):
     cols = vec_cols.shape[1]
-    total = jnp.sum(got[...], axis=0)
-    small = mm3(total, vec_cols[...], NT)
+    for part in range(got.shape[0]):
+        cols_t[part * HALF : (part + 1) * HALF, :] = got[part, HALF:, :]
+    vec = vectors(cols_t[...], -inv_s[...], lower[...], lax.axis_index("pcol") == 0)
+    vec_cols[...] = vec
+    total = jnp.sum(got[...], axis=0)[:HALF]
+    small = mm3(total, vec, NT)
     for dest in range(sent.shape[0]):
         sent[dest, :, :cols] = total
         sent[dest, :, cols:] = small
@@ -240,7 +237,7 @@
     rows_t = exchange(block_t, "pcol").reshape(NB, rows)
     (sent,) = call(gram_kernel, [(n_row, HALF, 2 * NB + rows)], rows_t)
     small, blocks = call(
-        sort_kernel, [(n_col, HALF, 5 * NB), (n_row, HALF, cols)], exchange(sent, "prow")
+        sort_kernel, [(n_col, HALF, 5 * NB), (HALF, cols)], exchange(sent, "prow")
     )
     band, inv_s, lower, tfac = call(
         factor_kernel,
@@ -250,15 +247,22 @@
         cost=pl.CostEstimate(flops=2 * 10**10, bytes_accessed=2**20, transcendentals=0),
         vmem=8 * 2**20,
     )
-    cols_t = exchange(blocks, "prow")
     vec_rows, sent = call(
-        product_kernel, [(NB, rows), (n_row, HALF, cols)], rows_t, matrix, inv_s, lower
-    )
-    (vec_cols,) = call(
-        column_kernel, [(NB, cols)], cols_t, inv_s, lower, scratch=[(NB, cols)]
-    )
-    (sent,) = call(
-        reduce_kernel, [(n_col, HALF, cols + NB)], exchange(sent, "prow"), vec_cols
+        product_kernel,
+        [(NB, rows), (n_row, SUB, cols)],
+        rows_t,
+        blocks,
+        matrix,
+        inv_s,
+        lower,
+    )
+    vec_cols, sent = call(
+        reduce_kernel,
+        [(NB, cols), (n_col, HALF, cols + NB)],
+        exchange(sent, "prow"),
+        inv_s,
+        lower,
+        scratch=[(NB, cols)],
     )
     wide = lane_ceil(cols + rows) + NB
     (sent,) = call(spread_kernel, [(n_row, HALF, wide)], exchange(sent, "pcol"))

time: 151 us -> 148 us (0.980)
  blocking collectives: 105 us -> 133 us
  waiting for transfers between devices: 18.7 us -> 0 us
  starting transfers between devices: 11 us -> 0 us
    all_to_all x5 -> x6, blocking collectives: 105 us -> 133 us  [exchange(): return lax.all_to_all(blocks, axis, 0, 0)]
    all_to_all x2 -> x0, waiting for transfers between devices: 18.7 us -> none  [exchange(): return lax.all_to_all(blocks, axis, 0, 0)]
    all_to_all x2 -> x0, starting transfers between devices: 11 us -> none  [exchange(): return lax.all_to_all(blocks, axis, 0, 0)]
    pallas_call x8 -> x7, Pallas kernels: 14.2 us -> 12.9 us  [call(): pl.pallas_call(kernel, out_shape=outs, scratch_shapes=[pltpu.VMEM(s, jnp....]
  transfers between devices with their start and end apart: 2 -> 0, of which waited for: 2 -> 0; matrix products, arithmetic and copies ran while one was open for 0% -> 0% of each run, Pallas kernels for 6% -> 0%
where the time goes in v7:
time: 148 us; the launch traced here: 147 us
  blocking collectives  133 us (90%)
  Pallas kernels  12.9 us (9%)
    all_to_all x6, blocking collectives, exchange(): return lax.all_to_all(blocks, axis, 0, 0)  133 us
    pallas_call x7, Pallas kernels, call(): pl.pallas_call(kernel, out_shape=outs, scratch_shapes=[pltpu.VMEM(s, jnp....  12.9 us

profile of v7, /device:TPU:1, one launch (start us, length us, event | category | flops | bytes accessed | tf_op | source)
XLA Modules:
  0.0 147.2 jit_solution(9632952656422832541)
XLA Ops:
  0.6 0.7 broadcast_in_dim.2
  1.4 21.2 %all_to_all.30 = f32[16,8,448]{2,1,0:T(8,128)S(1)} all-to-all(f32[16,8,448]{2,1,0:T(8,128)S(1)} %broadcast_in_dim.2), channel_id=1, replica_groups=mesh['prow'=32,'pcol'=16] {'pcol'}, dimensions={0} | all-to-all | bytes 458752 | tf_op jit(solution)/shard_map/all_to_all | solution.py:230
  22.5 0.4 shard_map.41
  22.9 25.0 %all_to_all.31.got = f32[32,4,704]{2,1,0:T(4,128)S(1)} all-to-all(f32[32,4,704]{2,1,0:T(4,128)S(1)} %shard_map.41), channel_id=1, replica_groups=mesh['prow'=32,'pcol'=16] {'prow'}, dimensions={0} | all-to-all | bytes 720896 | tf_op jit(solution)/shard_map/all_to_all | solution.py:230
  47.9 0.1 shard_map.42
  48.0 14.2 %all_to_all.32.got = f32[16,4,640]{2,1,0:T(4,128)S(1)} all-to-all(f32[16,4,640]{2,1,0:T(4,128)S(1)} %get-tuple-element.13), channel_id=1, replica_groups=mesh['prow'=32,'pcol'=16] {'pcol'}, dimensions={0} | all-to-all | bytes 327680 | tf_op jit(solution)/shard_map/all_to_all | solution.py:230
  62.1 0.0 copy-start
  62.1 6.8 %shard_map.43 = (f32[128,128]{1,0:T(8,128)}, f32[128,128]{1,0:T(8,128)S(1)}, f32[128,128]{1,0:T(8,128)S(1)}, f32[128,128]{1,0:T(8,128)S(1)}) custom-call(f32[16,4,640]{2,1,0:T(4,128)S(1)} %all_to_all.32.got), custom_call_target="tpu_custom_call" | custom-call | flops 20000000000 | bytes 1048576 | tf_op jit(solution)/shard_map/pallas_call | solution.py:220
  68.9 0.0 copy-done
  68.9 1.4 shard_map.44
  70.3 29.6 %all_to_all.33.got = f32[32,8,896]{2,1,0:T(8,128)S(1)} all-to-all(f32[32,8,896]{2,1,0:T(8,128)S(1)} %get-tuple-element.17), channel_id=1, replica_groups=mesh['prow'=32,'pcol'=16] {'prow'}, dimensions={0} | all-to-all | bytes 1835008 | tf_op jit(solution)/shard_map/all_to_all | solution.py:230
  99.9 1.2 shard_map.45
  101.1 15.9 %all_to_all.34.got = f32[16,4,1024]{2,1,0:T(4,128)S(1)} all-to-all(f32[16,4,1024]{2,1,0:T(4,128)S(1)} %get-tuple-element.19), channel_id=1, replica_groups=mesh['prow'=32,'pcol'=16] {'pcol'}, dimensions={0} | all-to-all | bytes 524288 | tf_op jit(solution)/shard_map/all_to_all | solution.py:230
  117.0 0.1 shard_map.46
  117.1 27.1 %all_to_all.35.got = f32[32,4,1536]{2,1,0:T(4,128)S(1)} all-to-all(f32[32,4,1536]{2,1,0:T(4,128)S(1)} %shard_map.46), channel_id=1, replica_groups=mesh['prow'=32,'pcol'=16] {'prow'}, dimensions={0} | all-to-all | bytes 1572864 | tf_op jit(solution)/shard_map/all_to_all | solution.py:230
  144.2 3.0 %shard_map.47 = f32[448,896]{1,0:T(8,128)} custom-call(f32[128,448]{1,0:T(8,128)S(1)} %get-tuple-element.16.vec_rows, f32[128,896]{1,0:T(8,128)S(1)} %get-tuple-element.18.vec_cols, f32[32,4,1536]{2,1,0:T(4,128)S(1)} %all_to_all.35.got, f32[448,896]{1,0:T(8,128)S(1)} %copy-done, f32[128,128]{1,0:T(8,128)S(1)} %get-tuple-element.20.tfac), custom_call_target="tpu_custom_call" | custom-call | tf_op jit(solution)/shard_map/pallas_call | solution.py:220
Async XLA Ops:
  62.1 6.8 %copy-start = (f32[448,896]{1,0:T(8,128)S(1)}, f32[448,896]{1,0:T(8,128)}, u32[]{:S(2)}) copy-start(f32[448,896]{1,0:T(8,128)} %matrix.3) | copy-start | bytes 4816900

commit v8 on v7

--- a/solution.py
+++ b/solution.py
@@ -77,8 +77,8 @@
     blocks[...] = both
 
 
-def vectors(panel_t, combine, low, is_first):
-    vec = mm(combine, first_rows_zeroed(panel_t, is_first), TN)
+def vectors(panel_t, combine, low, is_first, product=mm):
+    vec = product(combine, first_rows_zeroed(panel_t, is_first), TN)
     head = vec[:, :NB] + low.T * jnp.where(is_first, 1.0, 0.0)
     return jnp.concatenate([head, vec[:, NB:]], 1)
 
@@ -97,7 +97,7 @@
     cols = vec_cols.shape[1]
     for part in range(got.shape[0]):
         cols_t[part * HALF : (part + 1) * HALF, :] = got[part, HALF:, :]
-    vec = vectors(cols_t[...], -inv_s[...], lower[...], lax.axis_index("pcol") == 0)
+    vec = vectors(cols_t[...], -inv_s[...], lower[...], lax.axis_index("pcol") == 0, mm3)
     vec_cols[...] = vec
     total = jnp.sum(got[...], axis=0)[:HALF]
     small = mm3(total, vec, NT)
@@ -201,7 +201,7 @@
     tfac[...] = -mm(upper[...], mm(inv_l[...], inv_c[...]), NT)
 
 
-def update_kernel(vec_rows, vec_cols, got, matrix, tfac, out, moved):
+def update_kernel(vec_rows, vec_cols, got, matrix, tfac, out, moved, block, left_done):
     rows, cols = matrix.shape
     at = lane_ceil(cols + rows)
     for part in range(got.shape[0]):
@@ -212,7 +212,14 @@
     upd_cols = prod[:, :cols] - mm3(0.5 * (mid + mid.T), vec_cols[...])
     left = jnp.concatenate([vec_rows[...], prod[:, cols:]], 0)
     right = jnp.concatenate([upd_cols, vec_cols[...]], 0)
-    out[...] = matrix[...] - mm3(left, right, TN)
+    sends = []
+    for at, stripe in enumerate((slice(0, 3 * NB), slice(3 * NB, 5 * NB), slice(5 * NB, cols))):
+        block[:, stripe] = matrix[:, stripe] - mm3(left, right[:, stripe], TN)
+        send = pltpu.make_async_copy(block.at[:, stripe], out.at[:, stripe], left_done.at[at])
+        send.start()
+        sends.append(send)
+    for send in sends:
+        send.wait()
 
 
 def call(kernel, shapes, *args, scratch=(), cost=None, vmem=VMEM_BYTES):
@@ -266,16 +273,19 @@
     )
     wide = lane_ceil(cols + rows) + NB
     (sent,) = call(spread_kernel, [(n_row, HALF, wide)], exchange(sent, "pcol"))
-    (trailing,) = call(
+    vmem, hbm = pl.BlockSpec(memory_space=pltpu.VMEM), pl.BlockSpec(memory_space=pl.ANY)
+    trailing = pl.pallas_call(
         update_kernel,
-        [(rows, cols)],
-        vec_rows,
-        vec_cols,
-        exchange(sent, "prow"),
-        matrix,
-        tfac,
-        scratch=[(NB, wide)],
-    )
+        out_shape=jax.ShapeDtypeStruct((rows, cols), jnp.float32),
+        in_specs=[vmem] * 5,
+        out_specs=hbm,
+        scratch_shapes=[
+            pltpu.VMEM((NB, wide), jnp.float32),
+            pltpu.VMEM((rows, cols), jnp.float32),
+            pltpu.SemaphoreType.DMA((3,)),
+        ],
+        compiler_params=pltpu.CompilerParams(vmem_limit_bytes=VMEM_BYTES),
+    )(vec_rows, vec_cols, exchange(sent, "prow"), matrix, tfac)
     return (trailing, band)
 
 

time: 148 us -> 147 us (level)
    pallas_call x7 -> x6, Pallas kernels: 12.9 us -> 9.68 us  [call(): pl.pallas_call(kernel, out_shape=outs, scratch_shapes=[pltpu.VMEM(s, jnp....]
    pallas_call x0 -> x1, Pallas kernels: none -> 2.87 us  [local(): pl.pallas_call(update_kernel, out_shape=jax.ShapeDtypeStruct((rows, cols)...]
where the time goes in v8:
time: 147 us
  blocking collectives  133 us (90%)
  Pallas kernels  12.5 us (9%)
    all_to_all x6, blocking collectives, exchange(): return lax.all_to_all(blocks, axis, 0, 0)  133 us
    pallas_call x6, Pallas kernels, call(): pl.pallas_call(kernel, out_shape=outs, scratch_shapes=[pltpu.VMEM(s, jnp....  9.68 us

profile of v8, /device:TPU:1, one launch (start us, length us, event | category | flops | bytes accessed | tf_op | source)
XLA Modules:
  0.0 146.8 jit_solution(4957383551506741535)
XLA Ops:
  0.6 0.7 broadcast_in_dim.2
  1.4 21.2 %all_to_all.30 = f32[16,8,448]{2,1,0:T(8,128)S(1)} all-to-all(f32[16,8,448]{2,1,0:T(8,128)S(1)} %broadcast_in_dim.2), channel_id=1, replica_groups=mesh['prow'=32,'pcol'=16] {'pcol'}, dimensions={0} | all-to-all | bytes 458752 | tf_op jit(solution)/shard_map/all_to_all | solution.py:237
  22.5 0.4 shard_map.41
  22.9 25.0 %all_to_all.31.got = f32[32,4,704]{2,1,0:T(4,128)S(1)} all-to-all(f32[32,4,704]{2,1,0:T(4,128)S(1)} %shard_map.41), channel_id=1, replica_groups=mesh['prow'=32,'pcol'=16] {'prow'}, dimensions={0} | all-to-all | bytes 720896 | tf_op jit(solution)/shard_map/all_to_all | solution.py:237
  47.9 0.1 shard_map.42
  48.0 14.2 %all_to_all.32.got = f32[16,4,640]{2,1,0:T(4,128)S(1)} all-to-all(f32[16,4,640]{2,1,0:T(4,128)S(1)} %get-tuple-element.13), channel_id=1, replica_groups=mesh['prow'=32,'pcol'=16] {'pcol'}, dimensions={0} | all-to-all | bytes 327680 | tf_op jit(solution)/shard_map/all_to_all | solution.py:237
  62.1 0.0 copy-start
  62.1 6.8 %shard_map.43 = (f32[128,128]{1,0:T(8,128)}, f32[128,128]{1,0:T(8,128)S(1)}, f32[128,128]{1,0:T(8,128)S(1)}, f32[128,128]{1,0:T(8,128)S(1)}) custom-call(f32[16,4,640]{2,1,0:T(4,128)S(1)} %all_to_all.32.got), custom_call_target="tpu_custom_call" | custom-call | flops 20000000000 | bytes 1048576 | tf_op jit(solution)/shard_map/pallas_call | solution.py:227
  68.9 0.0 copy-done
  68.9 1.4 shard_map.44
  70.3 29.6 %all_to_all.33.got = f32[32,8,896]{2,1,0:T(8,128)S(1)} all-to-all(f32[32,8,896]{2,1,0:T(8,128)S(1)} %get-tuple-element.17), channel_id=1, replica_groups=mesh['prow'=32,'pcol'=16] {'prow'}, dimensions={0} | all-to-all | bytes 1835008 | tf_op jit(solution)/shard_map/all_to_all | solution.py:237
  99.9 0.9 shard_map.45
  100.8 15.9 %all_to_all.34.got = f32[16,4,1024]{2,1,0:T(4,128)S(1)} all-to-all(f32[16,4,1024]{2,1,0:T(4,128)S(1)} %get-tuple-element.19), channel_id=1, replica_groups=mesh['prow'=32,'pcol'=16] {'pcol'}, dimensions={0} | all-to-all | bytes 524288 | tf_op jit(solution)/shard_map/all_to_all | solution.py:237
  116.8 0.1 shard_map.46
  116.9 27.1 %all_to_all.35.got = f32[32,4,1536]{2,1,0:T(4,128)S(1)} all-to-all(f32[32,4,1536]{2,1,0:T(4,128)S(1)} %shard_map.46), channel_id=1, replica_groups=mesh['prow'=32,'pcol'=16] {'prow'}, dimensions={0} | all-to-all | bytes 1572864 | tf_op jit(solution)/shard_map/all_to_all | solution.py:237
  144.0 2.9 %shard_map.47 = f32[448,896]{1,0:T(8,128)} custom-call(f32[128,448]{1,0:T(8,128)S(1)} %get-tuple-element.16.vec_rows, f32[128,896]{1,0:T(8,128)S(1)} %get-tuple-element.18.vec_cols, f32[32,4,1536]{2,1,0:T(4,128)S(1)} %all_to_all.35.got, f32[448,896]{1,0:T(8,128)S(1)} %copy-done, f32[128,128]{1,0:T(8,128)S(1)} %get-tuple-element.20.tfac), custom_call_target="tpu_custom_call" | custom-call | tf_op jit(solution)/shard_map/pallas_call | solution.py:277
Async XLA Ops:
  62.1 6.8 %copy-start = (f32[448,896]{1,0:T(8,128)S(1)}, f32[448,896]{1,0:T(8,128)}, u32[]{:S(2)}) copy-start(f32[448,896]{1,0:T(8,128)} %matrix.3) | copy-start | bytes 4816900

commit v9 on v8

--- a/solution.py
+++ b/solution.py
@@ -86,7 +86,7 @@
 def product_kernel(rows_t, blocks, matrix, inv_s, lower, vec_rows, sent):
     vec = vectors(rows_t[...], -inv_s[...], lower[...], lax.axis_index("prow") == 0)
     vec_rows[...] = vec
-    part = mm(vec, matrix[...])
+    part = mm3(vec, matrix[...])
     block = blocks[...]
     for dest in range(sent.shape[0]):
         sent[dest, :HALF, :] = part[dest * HALF : (dest + 1) * HALF]

time: 147 us -> 147 us (level)
  no operation moved by 1% of the time
where the time goes in v9:
time: 147 us; the launch traced here: 146 us
  blocking collectives  133 us (90%)
  Pallas kernels  12.1 us (8%)
    all_to_all x6, blocking collectives, exchange(): return lax.all_to_all(blocks, axis, 0, 0)  133 us
    pallas_call x6, Pallas kernels, call(): pl.pallas_call(kernel, out_shape=outs, scratch_shapes=[pltpu.VMEM(s, jnp....  9.27 us

profile of v9, /device:TPU:1, one launch (start us, length us, event | category | flops | bytes accessed | tf_op | source)
XLA Modules:
  0.0 146.4 jit_solution(1089454636870454515)
XLA Ops:
  0.6 0.7 broadcast_in_dim.2
  1.4 21.2 %all_to_all.30 = f32[16,8,448]{2,1,0:T(8,128)S(1)} all-to-all(f32[16,8,448]{2,1,0:T(8,128)S(1)} %broadcast_in_dim.2), channel_id=1, replica_groups=mesh['prow'=32,'pcol'=16] {'pcol'}, dimensions={0} | all-to-all | bytes 458752 | tf_op jit(solution)/shard_map/all_to_all | solution.py:237
  22.5 0.4 shard_map.41
  22.9 25.0 %all_to_all.31.got = f32[32,4,704]{2,1,0:T(4,128)S(1)} all-to-all(f32[32,4,704]{2,1,0:T(4,128)S(1)} %shard_map.41), channel_id=1, replica_groups=mesh['prow'=32,'pcol'=16] {'prow'}, dimensions={0} | all-to-all | bytes 720896 | tf_op jit(solution)/shard_map/all_to_all | solution.py:237
  47.9 0.1 shard_map.42
  48.0 14.2 %all_to_all.32.got = f32[16,4,640]{2,1,0:T(4,128)S(1)} all-to-all(f32[16,4,640]{2,1,0:T(4,128)S(1)} %get-tuple-element.13), channel_id=1, replica_groups=mesh['prow'=32,'pcol'=16] {'pcol'}, dimensions={0} | all-to-all | bytes 327680 | tf_op jit(solution)/shard_map/all_to_all | solution.py:237
  62.1 0.0 copy-start
  62.1 6.8 %shard_map.43 = (f32[128,128]{1,0:T(8,128)}, f32[128,128]{1,0:T(8,128)S(1)}, f32[128,128]{1,0:T(8,128)S(1)}, f32[128,128]{1,0:T(8,128)S(1)}) custom-call(f32[16,4,640]{2,1,0:T(4,128)S(1)} %all_to_all.32.got), custom_call_target="tpu_custom_call" | custom-call | flops 20000000000 | bytes 1048576 | tf_op jit(solution)/shard_map/pallas_call | solution.py:227
  68.9 0.0 copy-done
  68.9 1.0 shard_map.44
  69.9 29.6 %all_to_all.33.got = f32[32,8,896]{2,1,0:T(8,128)S(1)} all-to-all(f32[32,8,896]{2,1,0:T(8,128)S(1)} %get-tuple-element.17), channel_id=1, replica_groups=mesh['prow'=32,'pcol'=16] {'prow'}, dimensions={0} | all-to-all | bytes 1835008 | tf_op jit(solution)/shard_map/all_to_all | solution.py:237
  99.5 0.9 shard_map.45
  100.4 15.9 %all_to_all.34.got = f32[16,4,1024]{2,1,0:T(4,128)S(1)} all-to-all(f32[16,4,1024]{2,1,0:T(4,128)S(1)} %get-tuple-element.19), channel_id=1, replica_groups=mesh['prow'=32,'pcol'=16] {'pcol'}, dimensions={0} | all-to-all | bytes 524288 | tf_op jit(solution)/shard_map/all_to_all | solution.py:237
  116.4 0.1 shard_map.46
  116.5 27.1 %all_to_all.35.got = f32[32,4,1536]{2,1,0:T(4,128)S(1)} all-to-all(f32[32,4,1536]{2,1,0:T(4,128)S(1)} %shard_map.46), channel_id=1, replica_groups=mesh['prow'=32,'pcol'=16] {'prow'}, dimensions={0} | all-to-all | bytes 1572864 | tf_op jit(solution)/shard_map/all_to_all | solution.py:237
  143.6 2.9 %shard_map.47 = f32[448,896]{1,0:T(8,128)} custom-call(f32[128,448]{1,0:T(8,128)S(1)} %get-tuple-element.16.vec_rows, f32[128,896]{1,0:T(8,128)S(1)} %get-tuple-element.18.vec_cols, f32[32,4,1536]{2,1,0:T(4,128)S(1)} %all_to_all.35.got, f32[448,896]{1,0:T(8,128)S(1)} %copy-done, f32[128,128]{1,0:T(8,128)S(1)} %get-tuple-element.20.tfac), custom_call_target="tpu_custom_call" | custom-call | tf_op jit(solution)/shard_map/pallas_call | solution.py:277
Async XLA Ops:
  62.1 6.8 %copy-start = (f32[448,896]{1,0:T(8,128)S(1)}, f32[448,896]{1,0:T(8,128)}, u32[]{:S(2)}) copy-start(f32[448,896]{1,0:T(8,128)} %matrix.3) | copy-start | bytes 4816900

commit v10 on v9

--- a/solution.py
+++ b/solution.py
@@ -77,8 +77,8 @@
     blocks[...] = both
 
 
-def vectors(panel_t, combine, low, is_first, product=mm):
-    vec = product(combine, first_rows_zeroed(panel_t, is_first), TN)
+def vectors(panel_t, combine, low, is_first):
+    vec = mm(combine, first_rows_zeroed(panel_t, is_first), TN)
     head = vec[:, :NB] + low.T * jnp.where(is_first, 1.0, 0.0)
     return jnp.concatenate([head, vec[:, NB:]], 1)
 
@@ -97,7 +97,7 @@
     cols = vec_cols.shape[1]
     for part in range(got.shape[0]):
         cols_t[part * HALF : (part + 1) * HALF, :] = got[part, HALF:, :]
-    vec = vectors(cols_t[...], -inv_s[...], lower[...], lax.axis_index("pcol") == 0, mm3)
+    vec = vectors(cols_t[...], -inv_s[...], lower[...], lax.axis_index("pcol") == 0)
     vec_cols[...] = vec
     total = jnp.sum(got[...], axis=0)[:HALF]
     small = mm3(total, vec, NT)

time: 147 us -> 147 us (level)
  no operation moved by 1% of the time
where the time goes in v10:
time: 147 us
  blocking collectives  133 us (90%)
  Pallas kernels  12.4 us (8%)
    all_to_all x6, blocking collectives, exchange(): return lax.all_to_all(blocks, axis, 0, 0)  133 us
    pallas_call x6, Pallas kernels, call(): pl.pallas_call(kernel, out_shape=outs, scratch_shapes=[pltpu.VMEM(s, jnp....  9.51 us

profile of v10, /device:TPU:1, one launch (start us, length us, event | category | flops | bytes accessed | tf_op | source)
XLA Modules:
  0.0 146.7 jit_solution(2708413262213135826)
XLA Ops:
  0.6 0.7 broadcast_in_dim.2
  1.4 21.2 %all_to_all.30 = f32[16,8,448]{2,1,0:T(8,128)S(1)} all-to-all(f32[16,8,448]{2,1,0:T(8,128)S(1)} %broadcast_in_dim.2), channel_id=1, replica_groups=mesh['prow'=32,'pcol'=16] {'pcol'}, dimensions={0} | all-to-all | bytes 458752 | tf_op jit(solution)/shard_map/all_to_all | solution.py:237
  22.5 0.4 shard_map.41
  22.9 25.0 %all_to_all.31.got = f32[32,4,704]{2,1,0:T(4,128)S(1)} all-to-all(f32[32,4,704]{2,1,0:T(4,128)S(1)} %shard_map.41), channel_id=1, replica_groups=mesh['prow'=32,'pcol'=16] {'prow'}, dimensions={0} | all-to-all | bytes 720896 | tf_op jit(solution)/shard_map/all_to_all | solution.py:237
  47.9 0.1 shard_map.42
  48.0 14.2 %all_to_all.32.got = f32[16,4,640]{2,1,0:T(4,128)S(1)} all-to-all(f32[16,4,640]{2,1,0:T(4,128)S(1)} %get-tuple-element.13), channel_id=1, replica_groups=mesh['prow'=32,'pcol'=16] {'pcol'}, dimensions={0} | all-to-all | bytes 327680 | tf_op jit(solution)/shard_map/all_to_all | solution.py:237
  62.1 0.0 copy-start
  62.1 6.8 %shard_map.43 = (f32[128,128]{1,0:T(8,128)}, f32[128,128]{1,0:T(8,128)S(1)}, f32[128,128]{1,0:T(8,128)S(1)}, f32[128,128]{1,0:T(8,128)S(1)}) custom-call(f32[16,4,640]{2,1,0:T(4,128)S(1)} %all_to_all.32.got), custom_call_target="tpu_custom_call" | custom-call | flops 20000000000 | bytes 1048576 | tf_op jit(solution)/shard_map/pallas_call | solution.py:227
  68.9 0.0 copy-done
  68.9 1.0 shard_map.44
  69.9 29.6 %all_to_all.33.got = f32[32,8,896]{2,1,0:T(8,128)S(1)} all-to-all(f32[32,8,896]{2,1,0:T(8,128)S(1)} %get-tuple-element.17), channel_id=1, replica_groups=mesh['prow'=32,'pcol'=16] {'prow'}, dimensions={0} | all-to-all | bytes 1835008 | tf_op jit(solution)/shard_map/all_to_all | solution.py:237
  99.5 1.2 shard_map.45
  100.7 15.9 %all_to_all.34.got = f32[16,4,1024]{2,1,0:T(4,128)S(1)} all-to-all(f32[16,4,1024]{2,1,0:T(4,128)S(1)} %get-tuple-element.19), channel_id=1, replica_groups=mesh['prow'=32,'pcol'=16] {'pcol'}, dimensions={0} | all-to-all | bytes 524288 | tf_op jit(solution)/shard_map/all_to_all | solution.py:237
  116.6 0.1 shard_map.46
  116.7 27.1 %all_to_all.35.got = f32[32,4,1536]{2,1,0:T(4,128)S(1)} all-to-all(f32[32,4,1536]{2,1,0:T(4,128)S(1)} %shard_map.46), channel_id=1, replica_groups=mesh['prow'=32,'pcol'=16] {'prow'}, dimensions={0} | all-to-all | bytes 1572864 | tf_op jit(solution)/shard_map/all_to_all | solution.py:237
  143.8 2.9 %shard_map.47 = f32[448,896]{1,0:T(8,128)} custom-call(f32[128,448]{1,0:T(8,128)S(1)} %get-tuple-element.16.vec_rows, f32[128,896]{1,0:T(8,128)S(1)} %get-tuple-element.18.vec_cols, f32[32,4,1536]{2,1,0:T(4,128)S(1)} %all_to_all.35.got, f32[448,896]{1,0:T(8,128)S(1)} %copy-done, f32[128,128]{1,0:T(8,128)S(1)} %get-tuple-element.20.tfac), custom_call_target="tpu_custom_call" | custom-call | tf_op jit(solution)/shard_map/pallas_call | solution.py:277
Async XLA Ops:
  62.1 6.8 %copy-start = (f32[448,896]{1,0:T(8,128)S(1)}, f32[448,896]{1,0:T(8,128)}, u32[]{:S(2)}) copy-start(f32[448,896]{1,0:T(8,128)} %matrix.3) | copy-start | bytes 4816900
